TPU v7x, 32 devices: a whole 2x2x4 slice. The times are simulated.
32 devices in a mesh: ctx: 4 (over z), head: 2 (over x), rep: 4 (over y, core).
Axes of the slice: x: 2, y: 2, z: 4, core: 2. Of those that a mesh axis runs over, the one named last changes fastest.
Arguments:
- queries: bfloat16 [4, 512, 8192], P('rep', 'ctx', 'head'), may hold values from -12 to 12
- keys: bfloat16 [4, 512, 1024], P('rep', 'ctx', 'head'), may hold values from -12 to 12
- values: bfloat16 [4, 512, 1024], P('rep', 'ctx', 'head'), may hold values from -6 to 6
- grad_out: bfloat16 [4, 512, 8192], P('rep', 'ctx', 'head'), may hold values from -90 to 90
- segment_ids: int32 [4, 512], P('rep'), may hold values from 0 to 7, never falling along the last dimension, each value on 1 to 256 neighbouring positions
- head_mask: float32 [64], P('head'), may hold values from 0.25 to 1
- ablated_heads: int32 [8], replicated, may hold values from 0 to 63, as said below
- w_query: bfloat16 [8192, 8192], P(('ctx', 'rep'), 'head'), may hold values from -0.0625 to 0.0625
- w_key: bfloat16 [8192, 1024], P(('ctx', 'rep'), 'head'), may hold values from -0.0625 to 0.0625
- w_value: bfloat16 [8192, 1024], P(('ctx', 'rep'), 'head'), may hold values from -0.0625 to 0.0625
Outputs:
- input_grad: bfloat16 [4, 512, 8192], P('rep', None, ('ctx', 'head'))
- mask_grad: float32 [64], P('head')
Inputs may be any that keep to these rules, and one draw needn't show every extreme that they name: `ablated_heads`: the 8 entries are all different.
All inputs are finite; a program needn't handle non-finite values.
Results may differ from a plain program's by a relative error of at most 0.02.
Values may be sent and summed in bfloat16 or wider, within the bound.
A program may use at most 192 MiB of HBM per device.

v0:
```python
import math

import jax
import jax.numpy as jnp
from jax import lax
from jax.sharding import PartitionSpec as P

DH = 128


NEG_FILL = -1e30


def shifted(block, axis, distance):
    devices = range(lax.axis_size(axis))
    route = [((i - distance) % len(devices), i) for i in devices]
    return lax.ppermute(block, axis, route)


def times_rows(left, right):
    return lax.dot_general(
        left, right, (((1,), (1,)), ((), ())), preferred_element_type=jnp.float32
    )


def block_scores(query_blocks, key_piece, query_pos, query_seg, key_seg, key_start):
    key_count = key_piece.shape[0]
    key_pos = key_start + jnp.arange(key_count, dtype=jnp.int32)
    allowed = (key_pos[None, :] <= query_pos[:, None]) & (key_seg[None, :] == query_seg[:, None])
    score_scale = 1.0 / math.sqrt(query_blocks.shape[-1])
    scores = (
        jnp.einsum("gjtc,kgc->gjtk", query_blocks, key_piece, preferred_element_type=jnp.float32)
        * score_scale
    )
    return (jnp.where(allowed, scores, NEG_FILL), allowed)


def rotate(key_value):
    return shifted(key_value, "ctx", -1)


def on_device(
    queries, keys, values, grad_out, segment_ids, head_mask, ablated_heads, w_query, w_key, w_value
):
    rows_dev = queries.shape[1]
    groups = keys.shape[2] // DH
    local_heads = head_mask.shape[0]
    per_group = local_heads // groups
    block_count = lax.axis_size("ctx")
    my_block = lax.axis_index("ctx")
    seq_len = block_count * rows_dev
    score_scale = 1.0 / math.sqrt(DH)
    all_seg = segment_ids[0]
    query_pos = my_block * rows_dev + jnp.arange(rows_dev, dtype=jnp.int32)
    query_seg = lax.dynamic_slice_in_dim(all_seg, my_block * rows_dev, rows_dev, 0)
    query_blocks = queries[0].reshape(rows_dev, groups, per_group, DH).transpose(1, 2, 0, 3)
    grad_blocks = grad_out[0].reshape(rows_dev, groups, per_group, DH).transpose(1, 2, 0, 3)
    head_ids = lax.axis_index("head") * local_heads + jnp.arange(local_heads, dtype=jnp.int32)
    ablate = jnp.any(head_ids[:, None] == ablated_heads[None, :], axis=1)
    head_scale = jnp.where(ablate, 0.0, head_mask).reshape(groups, per_group)
    key_value = jnp.stack([keys, values])

    def block_source(step_index):
        source = (my_block + step_index) % block_count
        key_start = source * rows_dev
        return (key_start, lax.dynamic_slice_in_dim(all_seg, key_start, rows_dev, 0))

    def forward_step(step_index, carried):
        moving, row_max, denominator, weighted = carried
        key_start, key_seg = block_source(step_index)
        softmax_state = (row_max, denominator, weighted)
        old_max, old_sum, old_weighted = softmax_state
        key_piece = moving[0, 0].reshape(rows_dev, groups, DH)
        value_piece = moving[1, 0].reshape(rows_dev, groups, DH)
        scores, allowed = block_scores(
            query_blocks, key_piece, query_pos, query_seg, key_seg, key_start
        )
        new_max = jnp.maximum(old_max, jnp.max(scores, axis=-1))
        exponent = jnp.where(allowed, jnp.exp(scores - new_max[..., None]), 0.0)
        rescale = jnp.exp(old_max - new_max)
        new_sum = old_sum * rescale + jnp.sum(exponent, axis=-1)
        new_weighted = old_weighted * rescale[..., None] + jnp.einsum(
            "gjtk,kgc->gjtc",
            exponent.astype(jnp.bfloat16),
            value_piece,
            preferred_element_type=jnp.float32,
        )
        softmax_state = (new_max, new_sum, new_weighted)
        return (rotate(moving),) + softmax_state

    start_max = jnp.full((groups, per_group, rows_dev), NEG_FILL, jnp.float32)
    start_sum = jnp.zeros((groups, per_group, rows_dev), jnp.float32)
    start_weighted = jnp.zeros((groups, per_group, rows_dev, DH), jnp.float32)
    forward_end = lax.fori_loop(
        0, block_count, forward_step, (key_value, start_max, start_sum, start_weighted)
    )
    row_max, denominator, weighted = (forward_end[1], forward_end[2], forward_end[3])
    log_total = row_max + jnp.log(denominator)
    head_out = (weighted / denominator[..., None]).astype(jnp.bfloat16)
    out_grad = (head_scale[:, :, None, None] * grad_blocks.astype(jnp.float32)).astype(jnp.bfloat16)
    out_dot = jnp.sum(out_grad.astype(jnp.float32) * head_out.astype(jnp.float32), axis=-1)

    def backward_step(step_index, carried):
        moving, key_grads, query_grad = carried
        key_start, key_seg = block_source(step_index)
        grad_state = (key_grads, query_grad)
        old_keys, old_query = grad_state
        key_piece = moving[0, 0].reshape(rows_dev, groups, DH)
        value_piece = moving[1, 0].reshape(rows_dev, groups, DH)
        scores, allowed = block_scores(
            query_blocks, key_piece, query_pos, query_seg, key_seg, key_start
        )
        probability = jnp.where(allowed, jnp.exp(scores - log_total[..., None]), 0.0)
        prob_grad = jnp.einsum(
            "gjtc,kgc->gjtk", out_grad, value_piece, preferred_element_type=jnp.float32
        )
        score_grad = (probability * (prob_grad - out_dot[..., None])).astype(jnp.bfloat16)
        value_term = jnp.einsum(
            "gjtk,gjtc->kgc",
            probability.astype(jnp.bfloat16),
            out_grad,
            preferred_element_type=jnp.float32,
        )
        key_term = (
            jnp.einsum(
                "gjtk,gjtc->kgc", score_grad, query_blocks, preferred_element_type=jnp.float32
            )
            * score_scale
        )
        new_query = (
            old_query
            + jnp.einsum(
                "gjtk,kgc->gjtc", score_grad, key_piece, preferred_element_type=jnp.float32
            )
            * score_scale
        )
        new_terms = jnp.stack([key_term, value_term]).reshape(old_keys.shape)
        grad_state = (old_keys + new_terms, new_query)
        passed = shifted(grad_state[0].astype(jnp.bfloat16), "ctx", -1).astype(jnp.float32)
        return (rotate(moving), passed, grad_state[1])

    backward_end = lax.fori_loop(
        0,
        block_count,
        backward_step,
        (
            key_value,
            jnp.zeros(key_value.shape, jnp.float32),
            jnp.zeros(query_blocks.shape, jnp.float32),
        ),
    )
    key_grads, query_grad = (backward_end[1], backward_end[2])
    query_rows = (
        query_grad.astype(jnp.bfloat16).transpose(2, 0, 1, 3).reshape(1, rows_dev, local_heads * DH)
    )
    key_rows = key_grads[0].astype(jnp.bfloat16)
    value_rows = key_grads[1].astype(jnp.bfloat16)
    mask_terms = jnp.sum(
        head_out.astype(jnp.float32) * grad_blocks.astype(jnp.float32), axis=(2, 3)
    ).reshape(local_heads)
    mask_grad = lax.psum(mask_terms, ("ctx", "rep")) / math.sqrt(lax.axis_size("rep") * seq_len)
    query_piece, key_piece, value_piece = lax.all_gather(
        (w_query, w_key, w_value), ("ctx", "rep"), axis=0, tiled=True
    )
    product = times_rows(query_rows[0], query_piece) + times_rows(key_rows[0], key_piece)
    product = product + times_rows(value_rows[0], value_piece)
    partial_value = product.astype(jnp.bfloat16)
    heads_count = lax.axis_size("head")
    columns = partial_value.shape[1]
    blocks = partial_value.reshape(
        rows_dev, block_count, heads_count, columns // (block_count * heads_count)
    )
    widened = lax.optimization_barrier(blocks).astype(jnp.float32)
    summed = lax.psum_scatter(widened.astype(jnp.bfloat16), "head", scatter_dimension=2, tiled=True)
    arrived = lax.all_to_all(summed, "ctx", split_axis=1, concat_axis=0, tiled=True)
    result = arrived.reshape(1, seq_len, -1)
    return (result, mask_grad)


def solution(mesh):
    placed = (
        P("rep", "ctx", "head"),
        P("rep", "ctx", "head"),
        P("rep", "ctx", "head"),
        P("rep", "ctx", "head"),
        P("rep", None),
        P("head"),
        P(),
        P(("ctx", "rep"), "head"),
        P(("ctx", "rep"), "head"),
        P(("ctx", "rep"), "head"),
    )
    return jax.shard_map(
        on_device,
        mesh=mesh,
        in_specs=placed,
        out_specs=(P("rep", None, ("ctx", "head")), P("head")),
        check_vma=False,
    )
```

profile of v0, /device:TPU:0, one launch (start us, length us, event | category | flops | bytes accessed | tf_op | source)
XLA Modules:
  0.0 693.7 jit_solution(18417028241824539484)
XLA Ops:
  15.3 67.9 %while.42 = (s32[]{:T(128)}, bf16[2,1,128,512]{2,3,1,0:T(8,128)(2,1)}, f32[4,8,128]{2,1,0:T(8,128)}, f32[4,8,128]{2,1,0:T(8,128)}, f32[4,8,128,128]{3,2,1,0:T(8,...) while((s32[]{:T(128)}, ...), condition=%wide.region_3.4_spmd.clone, body=%wide.region_0.3_spmd.clone.sunk | while | flops 276893952 | bytes 14488044 | solution.py:94
  16.3 5.0 collective-permute-start
  34.2 4.4 collective-permute-start
  51.1 4.4 collective-permute-start
  67.8 4.4 collective-permute-start
  92.4 114.9 %while.43 = (s32[]{:T(128)}, bf16[2,1,128,512]{2,3,1,0:T(8,128)(2,1)}, f32[2,1,128,512]{2,3,1,0:T(8,128)}, f32[4,8,128,128]{3,2,1,0:T(8,128)}, s32[]{:T(128)}, /...) while((s32[]{:T(128)}, ...), condition=%wide.region_7.8_spmd.clone, body=%wide.region_6.7_spmd.clone.sunk | while | flops 677626112 | bytes 26677736 | solution.py:142
  93.4 4.4 collective-permute-start.1
  107.3 12.6 %collective-permute-done.2 = bf16[2,1,128,512]{2,3,1,0:T(8,128)(2,1)} collective-permute-done((bf16[2,1,128,512]{2,3,1,0:T(8,128)(2,1)}, bf16[2,1,128,512]{2,3,1,0:T(8,128)(2,1)}, u32[]{:S(2)}, u32[]{:S(2)}) %collective-permute-start.2) | collective-permute-done | bytes 262176 | tf_op jit(solution)/shard_map/while/body/eval_jaxpr/ppermute | solution.py:17
  122.6 4.3 collective-permute-start.1
  137.8 10.9 %collective-permute-done.2 = bf16[2,1,128,512]{2,3,1,0:T(8,128)(2,1)} collective-permute-done((bf16[2,1,128,512]{2,3,1,0:T(8,128)(2,1)}, bf16[2,1,128,512]{2,3,1,0:T(8,128)(2,1)}, u32[]{:S(2)}, u32[]{:S(2)}) %collective-permute-start.2) | collective-permute-done | bytes 262176 | tf_op jit(solution)/shard_map/while/body/eval_jaxpr/ppermute | solution.py:17
  151.4 4.3 collective-permute-start.1
  166.7 10.5 %collective-permute-done.2 = bf16[2,1,128,512]{2,3,1,0:T(8,128)(2,1)} collective-permute-done((bf16[2,1,128,512]{2,3,1,0:T(8,128)(2,1)}, bf16[2,1,128,512]{2,3,1,0:T(8,128)(2,1)}, u32[]{:S(2)}, u32[]{:S(2)}) %collective-permute-start.2) | collective-permute-done | bytes 262176 | tf_op jit(solution)/shard_map/while/body/eval_jaxpr/ppermute | solution.py:17
  180.0 4.4 collective-permute-start.1
  195.2 10.3 %collective-permute-done.2 = bf16[2,1,128,512]{2,3,1,0:T(8,128)(2,1)} collective-permute-done((bf16[2,1,128,512]{2,3,1,0:T(8,128)(2,1)}, bf16[2,1,128,512]{2,3,1,0:T(8,128)(2,1)}, u32[]{:S(2)}, u32[]{:S(2)}) %collective-permute-start.2) | collective-permute-done | bytes 262176 | tf_op jit(solution)/shard_map/while/body/eval_jaxpr/ppermute | solution.py:17
  209.3 195.7 %all-gather.4.cloned.1.call-done = bf16[8192,4096]{1,0:T(8,128)(2,1)} async-done(((bf16[512,4096]{1,0:T(8,128)(2,1)}), bf16[8192,4096]{1,0:T(8,128)(2,1)}) %all-gather.4.cloned.1.call-update) | async-done | bytes 67108880 | tf_op jit(solution)/shard_map/all_gather | solution.py:162
  405.0 30.4 %fusion.27 = f32[128,8192]{1,0:T(8,128)} fusion(bf16[128,4096]{0,1:T(8,128)(2,1)S(1)} %bitcast.133, bf16[8192,4096]{1,0:T(8,128)(2,1)} %all-gather.4.cloned.1.call-done), kind=kOutput, calls=%fused_computation.57 | convolution fusion | flops 8589934592 | bytes 72351744 | tf_op jit(solution)/shard_map/dot_general | solution.py:21
  435.4 47.5 %all-gather.6.cloned.1.call-done = bf16[8192,512]{1,0:T(8,128)(2,1)} async-done(((bf16[512,512]{1,0:T(8,128)(2,1)}), bf16[8192,512]{1,0:T(8,128)(2,1)}) %all-gather.6.cloned.1.call-update) | async-done | bytes 8388624 | tf_op jit(solution)/shard_map/all_gather | solution.py:162
  482.9 9.5 %convolution_add_fusion.1 = f32[128,8192]{1,0:T(8,128)} fusion(f32[128,8192]{1,0:T(8,128)} %fusion.27, bf16[8192,512]{1,0:T(8,128)(2,1)} %all-gather.6.cloned.1.call-done, bf16[2,1,128,512]{2,3,1,0:T(8,128)(2,1)S(1)} %convert.6), kind=kOutput, calls=%fused_computation.37 | convolution fusion | flops 1074790400 | bytes 16908288 | tf_op jit(solution)/shard_map/dot_general | solution.py:21
  492.4 65.9 %all-gather.8.cloned.1.call-done = bf16[8192,512]{1,0:T(8,128)(2,1)} async-done(((bf16[512,512]{1,0:T(8,128)(2,1)}), bf16[8192,512]{1,0:T(8,128)(2,1)}) %all-gather.8.cloned.1.call-update) | async-done | bytes 8388624 | tf_op jit(solution)/shard_map/all_gather | solution.py:162
  558.3 7.4 %fusion.22 = bf16[128,8192]{1,0:T(8,128)(2,1)S(1)} fusion(f32[128,8192]{1,0:T(8,128)} %convolution_add_fusion.1, bf16[8192,512]{1,0:T(8,128)(2,1)} %all-gather.8.cloned.1.call-done, bf16[2,1,128,512]{2,3,1,0:T(8,128)(2,1)S(1)} %convert.6), kind=kOutput, calls=%fused_computation.38 | convolution fusion | flops 1075838976 | bytes 14811136 | tf_op jit(solution)/shard_map/dot_general | solution.py:21
  568.4 4.1 copy.67
  573.8 60.1 %all-reduce.3.cloned.1.call-done = bf16[128,4,2,1024]{3,0,2,1:T(8,128)(2,1)} async-done(((bf16[128,4,2,1024]{3,0,2,1:T(8,128)(2,1)}), bf16[128,4,2,1024]{3,0,2,1:T(8,128)(2,1)}) %all-reduce.3.cloned.1.call-update) | async-done | bytes 2097168
  636.8 4.6 all-to-all-start
  641.4 44.2 %psum.7 = f32[32]{0:T(128)S(1)} all-reduce(f32[32]{0:T(128)S(1)} %reshape.71), channel_id=1, replica_groups=mesh['ctx'=4,'head'=2,'rep'=4] {'ctx','rep'}, use_global_device_ids=true, to_apply=%region_10.11 | all-reduce | flops 32 | bytes 256 | tf_op jit(solution)/shard_map/psum | solution.py:161
  (219 shorter events, 130.0 us)
Async XLA Ops:
  7.2 397.8 %all-gather.4.cloned.1.call-start = ((), (), s32[]{:S(2)}) async-start(), calls=%async_computation.1 | async-start | bytes 71303168 | tf_op jit(solution)/shard_map/all_gather | solution.py:162
  7.9 475.0 %all-gather.6.cloned.1.call-start = ((), (), s32[]{:S(2)}) async-start(), calls=%async_computation.2 | async-start | bytes 8912896 | tf_op jit(solution)/shard_map/all_gather | solution.py:162
  8.7 549.6 %all-gather.8.cloned.1.call-start = ((), (), s32[]{:S(2)}) async-start(), calls=%async_computation.3 | async-start | bytes 8912896 | tf_op jit(solution)/shard_map/all_gather | solution.py:162
  9.4 624.5 %all-reduce.3.cloned.1.call-start = ((), (), s32[]{:S(2)}) async-start(), calls=%async_computation.4 | async-start | bytes 4194304
  16.3 16.9 %collective-permute-start = (bf16[2,1,128,512]{2,3,1,0:T(8,128)(2,1)S(1)}, bf16[2,1,128,512]{2,3,1,0:T(8,128)(2,1)}, u32[]{:S(2)}, u32[]{:S(2)}) collective-permute-start(bf16[2,1,128,512]{2,3,1,0:T(8,128)(2,1)S(1)} %copy.96), channel_id=1, source_target_pairs={{8,0},{16,8},{24,16},{0,24},{9,1},{17,9},{25,17},{1,25},{10,2},{18... | collective-permute-start | bytes 786440 | tf_op jit(solution)/shard_map/while/body/eval_jaxpr/ppermute | solution.py:17
  34.2 16.0 %collective-permute-start = (bf16[2,1,128,512]{2,3,1,0:T(8,128)(2,1)S(1)}, bf16[2,1,128,512]{2,3,1,0:T(8,128)(2,1)}, u32[]{:S(2)}, u32[]{:S(2)}) collective-permute-start(bf16[2,1,128,512]{2,3,1,0:T(8,128)(2,1)S(1)} %copy.96), channel_id=1, source_target_pairs={{8,0},{16,8},{24,16},{0,24},{9,1},{17,9},{25,17},{1,25},{10,2},{18... | collective-permute-start | bytes 786440 | tf_op jit(solution)/shard_map/while/body/eval_jaxpr/ppermute | solution.py:17
  40.7 3.1 copy-start.3
  40.7 3.1 copy-start.4
  40.7 3.1 copy-start.8
  51.1 15.7 %collective-permute-start = (bf16[2,1,128,512]{2,3,1,0:T(8,128)(2,1)S(1)}, bf16[2,1,128,512]{2,3,1,0:T(8,128)(2,1)}, u32[]{:S(2)}, u32[]{:S(2)}) collective-permute-start(bf16[2,1,128,512]{2,3,1,0:T(8,128)(2,1)S(1)} %copy.96), channel_id=1, source_target_pairs={{8,0},{16,8},{24,16},{0,24},{9,1},{17,9},{25,17},{1,25},{10,2},{18... | collective-permute-start | bytes 786440 | tf_op jit(solution)/shard_map/while/body/eval_jaxpr/ppermute | solution.py:17
  67.8 15.4 %collective-permute-start = (bf16[2,1,128,512]{2,3,1,0:T(8,128)(2,1)S(1)}, bf16[2,1,128,512]{2,3,1,0:T(8,128)(2,1)}, u32[]{:S(2)}, u32[]{:S(2)}) collective-permute-start(bf16[2,1,128,512]{2,3,1,0:T(8,128)(2,1)S(1)} %copy.96), channel_id=1, source_target_pairs={{8,0},{16,8},{24,16},{0,24},{9,1},{17,9},{25,17},{1,25},{10,2},{18... | collective-permute-start | bytes 786440 | tf_op jit(solution)/shard_map/while/body/eval_jaxpr/ppermute | solution.py:17
  74.3 3.1 copy-start.3
  83.2 3.1 copy-start.15
  83.2 3.2 copy-start.6
  93.4 28.3 %collective-permute-start.1 = (bf16[2,1,128,512]{2,3,1,0:T(8,128)(2,1)S(1)}, bf16[2,1,128,512]{2,3,1,0:T(8,128)(2,1)}, u32[]{:S(2)}, u32[]{:S(2)}) collective-permute-start(bf16[2,1,128,512]{2,3,1,0:T(8,128)(2,1)S(1)} %copy.110), channel_id=1, source_target_pairs={{8,0},{16,8},{24,16},{0,24},{9,1},{17,9},{25,17},{1,25},{10,2},{18... | collective-permute-start | bytes 786440 | tf_op jit(solution)/shard_map/while/body/eval_jaxpr/ppermute | solution.py:17
  105.5 14.4 %collective-permute-start.2 = (bf16[2,1,128,512]{2,3,1,0:T(8,128)(2,1)}, bf16[2,1,128,512]{2,3,1,0:T(8,128)(2,1)}, u32[]{:S(2)}, u32[]{:S(2)}) collective-permute-start(bf16[2,1,128,512]{2,3,1,0:T(8,128)(2,1)} %fusion.89), channel_id=1, source_target_pairs={{8,0},{16,8},{24,16},{0,24},{9,1},{17,9},{25,17},{1,25},{10,2},{18... | collective-permute-start | bytes 786440 | tf_op jit(solution)/shard_map/while/body/eval_jaxpr/ppermute | solution.py:17
  122.6 27.9 %collective-permute-start.1 = (bf16[2,1,128,512]{2,3,1,0:T(8,128)(2,1)S(1)}, bf16[2,1,128,512]{2,3,1,0:T(8,128)(2,1)}, u32[]{:S(2)}, u32[]{:S(2)}) collective-permute-start(bf16[2,1,128,512]{2,3,1,0:T(8,128)(2,1)S(1)} %copy.110), channel_id=1, source_target_pairs={{8,0},{16,8},{24,16},{0,24},{9,1},{17,9},{25,17},{1,25},{10,2},{18... | collective-permute-start | bytes 786440 | tf_op jit(solution)/shard_map/while/body/eval_jaxpr/ppermute | solution.py:17
  134.4 14.3 %collective-permute-start.2 = (bf16[2,1,128,512]{2,3,1,0:T(8,128)(2,1)}, bf16[2,1,128,512]{2,3,1,0:T(8,128)(2,1)}, u32[]{:S(2)}, u32[]{:S(2)}) collective-permute-start(bf16[2,1,128,512]{2,3,1,0:T(8,128)(2,1)} %fusion.89), channel_id=1, source_target_pairs={{8,0},{16,8},{24,16},{0,24},{9,1},{17,9},{25,17},{1,25},{10,2},{18... | collective-permute-start | bytes 786440 | tf_op jit(solution)/shard_map/while/body/eval_jaxpr/ppermute | solution.py:17
  151.4 27.6 %collective-permute-start.1 = (bf16[2,1,128,512]{2,3,1,0:T(8,128)(2,1)S(1)}, bf16[2,1,128,512]{2,3,1,0:T(8,128)(2,1)}, u32[]{:S(2)}, u32[]{:S(2)}) collective-permute-start(bf16[2,1,128,512]{2,3,1,0:T(8,128)(2,1)S(1)} %copy.110), channel_id=1, source_target_pairs={{8,0},{16,8},{24,16},{0,24},{9,1},{17,9},{25,17},{1,25},{10,2},{18... | collective-permute-start | bytes 786440 | tf_op jit(solution)/shard_map/while/body/eval_jaxpr/ppermute | solution.py:17
  163.3 13.9 %collective-permute-start.2 = (bf16[2,1,128,512]{2,3,1,0:T(8,128)(2,1)}, bf16[2,1,128,512]{2,3,1,0:T(8,128)(2,1)}, u32[]{:S(2)}, u32[]{:S(2)}) collective-permute-start(bf16[2,1,128,512]{2,3,1,0:T(8,128)(2,1)} %fusion.89), channel_id=1, source_target_pairs={{8,0},{16,8},{24,16},{0,24},{9,1},{17,9},{25,17},{1,25},{10,2},{18... | collective-permute-start | bytes 786440 | tf_op jit(solution)/shard_map/while/body/eval_jaxpr/ppermute | solution.py:17
  180.0 27.4 %collective-permute-start.1 = (bf16[2,1,128,512]{2,3,1,0:T(8,128)(2,1)S(1)}, bf16[2,1,128,512]{2,3,1,0:T(8,128)(2,1)}, u32[]{:S(2)}, u32[]{:S(2)}) collective-permute-start(bf16[2,1,128,512]{2,3,1,0:T(8,128)(2,1)S(1)} %copy.110), channel_id=1, source_target_pairs={{8,0},{16,8},{24,16},{0,24},{9,1},{17,9},{25,17},{1,25},{10,2},{18... | collective-permute-start | bytes 786440 | tf_op jit(solution)/shard_map/while/body/eval_jaxpr/ppermute | solution.py:17
  191.9 13.7 %collective-permute-start.2 = (bf16[2,1,128,512]{2,3,1,0:T(8,128)(2,1)}, bf16[2,1,128,512]{2,3,1,0:T(8,128)(2,1)}, u32[]{:S(2)}, u32[]{:S(2)}) collective-permute-start(bf16[2,1,128,512]{2,3,1,0:T(8,128)(2,1)} %fusion.89), channel_id=1, source_target_pairs={{8,0},{16,8},{24,16},{0,24},{9,1},{17,9},{25,17},{1,25},{10,2},{18... | collective-permute-start | bytes 786440 | tf_op jit(solution)/shard_map/while/body/eval_jaxpr/ppermute | solution.py:17
  633.8 7.5 %copy-start.13 = (f32[4,8]{1,0:T(4,128)S(1)}, f32[4,8]{1,0:T(4,128)}, u32[]{:S(2)}) copy-start(f32[4,8]{1,0:T(4,128)} %get-tuple-element.658) | copy-start | bytes 388
  636.8 49.4 %all-to-all-start = ((bf16[128,4,1,1024]{3,0,2,1:T(8,128)(2,1)}), bf16[128,4,1,1024]{3,0,2,1:T(8,128)(2,1)S(1)}, u32[]{:S(2)}, u32[]{:S(2)}) async-start(bf16[128,4,1,1024]{3,0,2,1:T(8,128)(2,1)} %constant_dynamic-slice_fusion), calls=%async_computation | async-start | bytes 2097152 | tf_op jit(solution)/shard_map/all_to_all | solution.py:175
  (28 other events, 48.9 us)
Sparse Core Ops, SparseCore 0:
  9.6 395.3 all-gather.3
  407.1 75.7 all-gather.5
  485.1 73.1 all-gather.7
  572.7 61.1 all-reduce.2
where the time goes:
time: 696 us; the launch traced here: 694 us
  waiting for transfers between devices  421 us (60%)
  matrix products  94 us (14%)
  local copies, waits for them, and re-layouts  51.9 us (7%)
  blocking collectives  44.2 us (6%)
  starting transfers between devices  40.3 us (6%)
  other arithmetic  28.3 us (4%)
  between operations  13.9 us (2%)
    all_gather x3, waiting for transfers between devices, on_device(): lax.all_gather((w_query, w_key, w_value), ('ctx', 'rep'), axis=0, tiled=T...  309 us
    unnamed x5, waiting for transfers between devices  62.2 us
    ppermute x12, waiting for transfers between devices, shifted(): return lax.ppermute(block, axis, route)  49.3 us
    dot_general x3, matrix products, times_rows(): lax.dot_general(left, right, (((1,), (1,)), ((), ())), preferred_element_...  47.3 us
    psum x1, blocking collectives, on_device(): lax.psum(mask_terms, ('ctx', 'rep'))  44.2 us
    ppermute x12, starting transfers between devices, shifted(): return lax.ppermute(block, axis, route)  35.5 us
    while x60, local copies, waits for them, and re-layouts  16.9 us
  transfers between devices with their start and end apart: 17, of which 12 were waited for; matrix products, arithmetic and copies ran while one was open for 21% of the time, Pallas kernels for 0%

commit v1 on v0

v1 whole, which is shorter than its diff:
```python
import functools
import math

import jax
import jax.numpy as jnp
from jax import lax
from jax.experimental import pallas as pl
from jax.experimental.pallas import tpu as pltpu
from jax.sharding import PartitionSpec as P

DH = 128
NEG_FILL = -1e30


def contract(left, right, left_dim, right_dim):
    return lax.dot_general(
        left, right, (((left_dim,), (right_dim,)), ((), ())), preferred_element_type=jnp.float32
    )


def attention_kernel(
    per_group, scale_ref, query_ref, grad_ref, key_ref, value_ref, row_seg_ref, key_seg_ref,
    dq_ref, dk_ref, dv_ref, mask_ref,
):
    rows, span = query_ref.shape[0], key_ref.shape[0]
    group = pl.program_id(0)
    score_scale = 1.0 / math.sqrt(DH)
    row_place = lax.broadcasted_iota(jnp.int32, (rows, span), 0) + (span - rows)
    key_place = lax.broadcasted_iota(jnp.int32, (rows, span), 1)
    allowed = (key_place <= row_place) & (key_seg_ref[...] == row_seg_ref[...])
    key, value = key_ref[...], value_ref[...]
    key_total = jnp.zeros((span, DH), jnp.float32)
    value_total = jnp.zeros((span, DH), jnp.float32)
    for j in range(per_group):
        columns = pl.ds(j * DH, DH)
        query = query_ref[:, columns]
        grad = grad_ref[:, columns].astype(jnp.float32)
        scores = jnp.where(allowed, contract(query, key, 1, 1) * score_scale, NEG_FILL)
        row_max = jnp.max(scores, axis=-1, keepdims=True)
        exponent = jnp.exp(scores - row_max)
        inverse = 1.0 / jnp.sum(exponent, axis=-1, keepdims=True)
        head_out = contract(exponent.astype(jnp.bfloat16), value, 1, 0) * inverse
        head_out = head_out.astype(jnp.bfloat16).astype(jnp.float32)
        out_grad = (scale_ref[group * per_group + j] * grad).astype(jnp.bfloat16)
        out_dot = jnp.sum(out_grad.astype(jnp.float32) * head_out, axis=-1, keepdims=True)
        probability = exponent * inverse
        prob_grad = contract(out_grad, value, 1, 1)
        score_grad = (probability * (prob_grad - out_dot)).astype(jnp.bfloat16)
        dq_ref[:, columns] = (contract(score_grad, key, 1, 0) * score_scale).astype(jnp.bfloat16)
        key_total = key_total + contract(score_grad, query, 0, 0)
        value_total = value_total + contract(probability.astype(jnp.bfloat16), out_grad, 0, 0)
        mask_ref[0, pl.ds(j, 1), :] = jnp.sum(head_out * grad, axis=0, keepdims=True)
    dk_ref[...] = (key_total * score_scale).astype(jnp.bfloat16)
    dv_ref[...] = value_total.astype(jnp.bfloat16)


def attention(scale, query, grad, key, value, row_seg, key_seg):
    rows, width = query.shape
    span, narrow = key.shape
    groups = narrow // DH
    per_group = width // narrow
    wide = pl.BlockSpec((rows, per_group * DH), lambda g: (0, g))
    thin = pl.BlockSpec((span, DH), lambda g: (0, g))
    return pl.pallas_call(
        functools.partial(attention_kernel, per_group),
        grid=(groups,),
        in_specs=[
            pl.BlockSpec(memory_space=pltpu.SMEM), wide, wide, thin, thin,
            pl.BlockSpec((rows, 1), lambda g: (0, 0)), pl.BlockSpec((1, span), lambda g: (0, 0)),
        ],
        out_specs=[wide, thin, thin, pl.BlockSpec((1, per_group, DH), lambda g: (g, 0, 0))],
        out_shape=[
            jax.ShapeDtypeStruct((rows, width), jnp.bfloat16),
            jax.ShapeDtypeStruct((span, narrow), jnp.bfloat16),
            jax.ShapeDtypeStruct((span, narrow), jnp.bfloat16),
            jax.ShapeDtypeStruct((groups, per_group, DH), jnp.float32),
        ],
        compiler_params=pltpu.CompilerParams(vmem_limit_bytes=40 * 1024 * 1024),
        cost_estimate=pl.CostEstimate(
            flops=12 * rows * span * width, bytes_accessed=6 * rows * width,
            transcendentals=rows * span * groups * per_group,
        ),
        name="attention",
    )(scale, query, grad, key, value, row_seg, key_seg)


def moved(block, distance):
    count = lax.axis_size("ctx")
    route = [(i, i + distance) for i in range(count) if 0 <= i + distance < count]
    return lax.ppermute(block, "ctx", route)


def swapped(block, flip):
    return lax.ppermute(block, "rep", [(i, i ^ flip) for i in range(lax.axis_size("rep"))])


def half_columns(arrays, half):
    parts = []
    for array in arrays:
        width = array.shape[1] // 2
        parts.append(lax.dynamic_slice_in_dim(array, half * width, width, 1))
    return jnp.concatenate(parts, axis=1)


def in_order(mine, other, place):
    first = place == 0
    return jnp.stack([jnp.where(first, mine, other), jnp.where(first, other, mine)])


def on_device(
    queries, keys, values, grad_out, segment_ids, head_mask, ablated_heads, w_query, w_key, w_value
):
    rows_dev = queries.shape[1]
    local_heads = head_mask.shape[0]
    block_count = lax.axis_size("ctx")
    my_block = lax.axis_index("ctx")
    rep_count, rep = lax.axis_size("rep"), lax.axis_index("rep")
    high, low = rep // 2, rep % 2
    seq_len = block_count * rows_dev
    narrow = keys.shape[2]
    before = min(block_count - 1, (seq_len // 2 + rows_dev - 2) // rows_dev)
    span = (before + 1) * rows_dev

    key_value = jnp.concatenate([keys[0], values[0]], axis=1)
    window = [moved(key_value, d) for d in range(before, 0, -1)] + [key_value]
    window = jnp.concatenate(window, axis=0)
    padded = jnp.concatenate(
        [jnp.full((before * rows_dev,), -1, jnp.int32), segment_ids[0]], axis=0
    )
    key_seg = lax.dynamic_slice_in_dim(padded, my_block * rows_dev, span, 0)
    row_seg = key_seg[before * rows_dev :]

    weights = (w_query, w_key, w_value)
    weight_mine = half_columns(weights, high)
    weight_other = swapped(half_columns(weights, 1 - high), 2)
    weight_pair = in_order(weight_mine, weight_other, high)
    weight_far = swapped(weight_pair, 1)

    head_ids = lax.axis_index("head") * local_heads + jnp.arange(local_heads, dtype=jnp.int32)
    ablate = jnp.any(head_ids[:, None] == ablated_heads[None, :], axis=1)
    head_scale = jnp.where(ablate, 0.0, head_mask)
    dq, dk, dv, mask_rows = attention(
        head_scale, queries[0], grad_out[0], window[:, :narrow], window[:, narrow:],
        row_seg[:, None], key_seg[None, :],
    )
    mask_terms = jnp.sum(mask_rows, axis=2).reshape(local_heads)
    mask_grad = lax.psum(mask_terms, ("ctx", "rep")) / math.sqrt(rep_count * seq_len)

    pair = jnp.concatenate([dk, dv], axis=1)
    total = pair[before * rows_dev :].astype(jnp.float32)
    for d in range(1, before + 1):
        piece = pair[(before - d) * rows_dev : (before - d + 1) * rows_dev]
        total = total + moved(piece, -d).astype(jnp.float32)
    total = total.astype(jnp.bfloat16)
    grads = (dq, total[:, :narrow], total[:, narrow:])
    grad_mine = half_columns(grads, high)
    grad_other = swapped(half_columns(grads, 1 - high), 2)
    grad_pair = in_order(grad_mine, grad_other, high)
    tokens = lax.all_gather(grad_pair, "ctx", axis=1, tiled=True)
    tokens = tokens.reshape(2 * seq_len, -1)
    weight_all = jnp.stack([
        jnp.where(low == 0, weight_pair, weight_far), jnp.where(low == 0, weight_far, weight_pair)
    ], axis=1)
    weight_all = weight_all.reshape(-1, weight_all.shape[-1])
    partial = contract(tokens, weight_all, 1, 1).astype(jnp.bfloat16)
    heads_count = lax.axis_size("head")
    head = lax.axis_index("head")
    partial = partial.reshape(2, seq_len, heads_count, -1)

    def piece_for(prompt, column):
        taken = lax.dynamic_slice_in_dim(partial, prompt, 1, 0)
        return lax.dynamic_slice_in_dim(taken, column, 1, 2)[0, :, 0]

    result = piece_for(high, head).astype(jnp.float32)
    for flip in range(2):
        for shift in range(heads_count):
            if flip == 0 and shift == 0:
                continue
            route = []
            for h in range(heads_count):
                for r in range(rep_count):
                    target = ((h + shift) % heads_count) * rep_count + (r ^ (2 * flip))
                    route.append((h * rep_count + r, target))
            sent = piece_for(high ^ flip, (head + shift) % heads_count)
            result = result + lax.ppermute(sent, ("head", "rep"), route).astype(jnp.float32)
    return (result.astype(jnp.bfloat16)[None], mask_grad)


def solution(mesh):
    placed = (
        P("rep", "ctx", "head"),
        P("rep", "ctx", "head"),
        P("rep", "ctx", "head"),
        P("rep", "ctx", "head"),
        P("rep", None),
        P("head"),
        P(),
        P(("ctx", "rep"), "head"),
        P(("ctx", "rep"), "head"),
        P(("ctx", "rep"), "head"),
    )
    return jax.shard_map(
        on_device,
        mesh=mesh,
        in_specs=placed,
        out_specs=(P("rep", None, ("ctx", "head")), P("head")),
        check_vma=False,
    )
```

time: 696 us -> 352 us (0.51)
  waiting for transfers between devices: 421 us -> 152 us
  matrix products: 94 us -> 16.7 us
  local copies, waits for them, and re-layouts: 51.9 us -> 28.8 us
  blocking collectives: 44.2 us -> 66 us
  starting transfers between devices: 40.3 us -> 20.4 us
  Pallas kernels: 0 us -> 19.4 us
    all_gather x3 -> x1, waiting for transfers between devices: 309 us -> 75.3 us  [on_device(): tokens = lax.all_gather(grad_pair, 'ctx', axis=1, tiled=True)]
    dot_general x31 -> x1, matrix products: 94 us -> 16.7 us  [contract(): lax.dot_general(left, right, (((left_dim,), (right_dim,)), ((), ())), pre...]
    unnamed x5 -> x1, waiting for transfers between devices: 62.2 us -> 0.02 us
    ppermute x12 -> x10, waiting for transfers between devices: 49.3 us -> 77 us  [the longest x3 53.2 us: swapped(): lax.ppermute(block, 'rep', [(i, i ^ flip) for i in range(lax.axis_size('r...]
    another operation x2 -> x6, other arithmetic: 0.79 us -> 25.3 us  [the longest x2 17 us: on_device(): jnp.stack([jnp.where(low == 0, weight_pair, weight_far), jnp.where(low ==...]
    psum x1, blocking collectives: 44.2 us -> 66 us  [on_device(): lax.psum(mask_terms, ('ctx', 'rep')) / math.sqrt(rep_count * seq_len)]
    while x62 -> x0, local copies, waits for them, and re-layouts: 21.7 us -> none
    pallas_call x0 -> x1, Pallas kernels: none -> 19.4 us  [attention(): pl.pallas_call(functools.partial(attention_kernel, per_group), grid=(grou...]
  transfers between devices with their start and end apart: 17 -> 11, of which waited for: 12 -> 5; matrix products, arithmetic and copies ran while one was open for 21% -> 10% of each run, Pallas kernels for 0% -> 0%
where the time goes in v1:
time: 352 us
  waiting for transfers between devices  152 us (43%)
  blocking collectives  66 us (19%)
  other arithmetic  33.9 us (10%)
  local copies, waits for them, and re-layouts  28.8 us (8%)
  starting transfers between devices  20.4 us (6%)
  Pallas kernels  19.4 us (6%)
  matrix products  16.7 us (5%)
  between operations  14.3 us (4%)
    all_gather x1, waiting for transfers between devices, on_device(): tokens = lax.all_gather(grad_pair, 'ctx', axis=1, tiled=True)  75.3 us
    psum x1, blocking collectives, on_device(): lax.psum(mask_terms, ('ctx', 'rep')) / math.sqrt(rep_count * seq_len)  66 us
    ppermute x3, waiting for transfers between devices, swapped(): lax.ppermute(block, 'rep', [(i, i ^ flip) for i in range(lax.axis_size('r...  53.2 us
    ppermute x4, waiting for transfers between devices, moved(): return lax.ppermute(block, 'ctx', route)  23.8 us
    pallas_call x1, Pallas kernels, attention(): pl.pallas_call(functools.partial(attention_kernel, per_group), grid=(grou...  19.4 us
    another operation x2, other arithmetic, on_device(): jnp.stack([jnp.where(low == 0, weight_pair, weight_far), jnp.where(low ==...  17 us
    dot_general x1, matrix products, contract(): lax.dot_general(left, right, (((left_dim,), (right_dim,)), ((), ())), pre...  16.7 us
    ppermute x4, starting transfers between devices, moved(): return lax.ppermute(block, 'ctx', route)  13.7 us
  transfers between devices with their start and end apart: 11, of which 5 were waited for; matrix products, arithmetic and copies ran while one was open for 10% of the time, Pallas kernels for 0%

profile of v1, /device:TPU:0, one launch (start us, length us, event | category | flops | bytes accessed | tf_op | source)
XLA Modules:
  0.0 351.9 jit_solution(13788462205863130895)
XLA Ops:
  7.2 1.7 pad_maximum_fusion.7
  8.9 6.6 %collective-permute-start = (bf16[128,1024]{1,0:T(8,128)(2,1)}, bf16[128,1024]{1,0:T(8,128)(2,1)}, u32[]{:S(2)}, u32[]{:S(2)}) collective-permute-start(bf16[128,1024]{1,0:T(8,128)(2,1)} %pad_maximum_fusion.7), channel_id=1, source_target_pairs={{0,16},{8,24},{1,17},{9,25},{2,18},{10,26},{3,19},{11,27},{4,20},{... | collective-permute-start | bytes 786440 | tf_op jit(solution)/shard_map/ppermute | solution.py:90
  15.5 4.2 %collective-permute-start.1 = (bf16[128,1024]{1,0:T(8,128)(2,1)}, bf16[128,1024]{1,0:T(8,128)(2,1)}, u32[]{:S(2)}, u32[]{:S(2)}) collective-permute-start(bf16[128,1024]{1,0:T(8,128)(2,1)} %pad_maximum_fusion.7), channel_id=1, source_target_pairs={{0,8},{8,16},{16,24},{1,9},{9,17},{17,25},{2,10},{10,18},{18,26},{... | collective-permute-start | bytes 786440 | tf_op jit(solution)/shard_map/ppermute | solution.py:90
  20.5 4.9 %constant_dynamic-slice_fusion.9 = (bf16[512,2048]{1,0:T(8,128)(2,1)}, bf16[512,2048]{1,0:T(8,128)(2,1)}) fusion(bf16[512,4096]{1,0:T(8,128)(2,1)} %param.17, s32[]{:T(128)S(6)} %select_n.116, s32[]{:T(128)S(6)} %select_n.118), kind=kLoop, calls=%fused_computation.38 | loop fusion | bytes 8388616 | tf_op jit(solution)/shard_map/dynamic_slice | solution.py:101
  27.7 19.4 %attention.1 = (bf16[128,4096]{1,0:T(8,128)(2,1)S(1)}, bf16[384,512]{1,0:T(8,128)(2,1)S(1)}, bf16[384,512]{1,0:T(8,128)(2,1)S(1)}, f32[4,8,128]{2,1,0:T(8,128)S(1)}) custom-call(f32[32]{0:T(128)S(1)} %broadcast_select_fusion.scale_ref, bf16[128,4096]{1,0:T(8,128)(2,1)S(1)} %bitcast.41, bf16[128,4096]{1,0:T(8,128)(2,1)S(1)} %bitcast.42, ...), custom_call_target="tpu_custom_call" | custom-call | flops 2415919104 | bytes 3145728 | tf_op jit(solution)/shard_map/attention/pallas_call | solution.py:64
  48.7 1.5 collective-permute-start.3
  50.4 1.6 collective-permute-start.5
  52.0 10.6 %collective-permute-done.2 = bf16[128,1024]{1,0:T(8,128)(2,1)S(1)} collective-permute-done((bf16[128,1024]{1,0:T(8,128)(2,1)S(1)}, bf16[128,1024]{1,0:T(8,128)(2,1)S(1)}, u32[]{:S(2)}, u32[]{:S(2)}) %collective-permute-start.2) | collective-permute-done | bytes 262176 | tf_op jit(solution)/shard_map/ppermute | solution.py:90
  62.7 13.1 %collective-permute-done.3 = bf16[128,1024]{1,0:T(8,128)(2,1)S(1)} collective-permute-done((bf16[128,1024]{1,0:T(8,128)(2,1)S(1)}, bf16[128,1024]{1,0:T(8,128)(2,1)S(1)}, u32[]{:S(2)}, u32[]{:S(2)}) %collective-permute-start.3) | collective-permute-done | bytes 262176 | tf_op jit(solution)/shard_map/ppermute | solution.py:90
  76.9 1.5 collective-permute-start.4
  78.4 44.2 %collective-permute-done.4 = bf16[128,2560]{1,0:T(8,128)(2,1)} collective-permute-done((bf16[128,2560]{1,0:T(8,128)(2,1)}, bf16[128,2560]{1,0:T(8,128)(2,1)}, u32[]{:S(2)}, u32[]{:S(2)}) %collective-permute-start.4) | collective-permute-done | bytes 655392 | tf_op jit(solution)/shard_map/ppermute | solution.py:94
  125.2 2.8 select_bitcast_fusion.3
  128.0 3.0 pad_maximum_fusion.1
  131.0 9.0 %collective-permute-done.6 = bf16[2,512,2560]{2,1,0:T(8,128)(2,1)} collective-permute-done((bf16[2,512,2560]{2,1,0:T(8,128)(2,1)}, bf16[2,512,2560]{2,1,0:T(8,128)(2,1)}, u32[]{:S(2)}, u32[]{:S(2)}) %collective-permute-start.6) | collective-permute-done | bytes 5242912 | tf_op jit(solution)/shard_map/ppermute | solution.py:94
  140.0 8.1 %select_bitcast_fusion.1 = (bf16[2,1,512,2560]{3,2,1,0:T(8,128)(2,1)}, bf16[2,1,512,2560]{3,2,1,0:T(8,128)(2,1)}) fusion(bf16[2,512,2560]{2,1,0:T(8,128)(2,1)} %collective-permute-done.6, pred[]{:T(512)S(6)} %eq.30, bf16[1,512,2560]{2,1,0:T(8,128)(2,1)} %copy-done.2, bf16[1,512,2560]{2,1,0:T(8,128)(2,1)S(1)} %get-tuple-element.12), kind=kLoop, calls=%fused_computation.3 | loop fusion | flops 7864320 | bytes 20971520 | tf_op jit(solution)/shard_map/stack | solution.py:161
  148.2 8.9 %pad_maximum_fusion = bf16[2,2,512,2560]{3,2,1,0:T(8,128)(2,1)} fusion(bf16[2,1,512,2560]{3,2,1,0:T(8,128)(2,1)} %get-tuple-element.11, bf16[2,1,512,2560]{3,2,1,0:T(8,128)(2,1)} %get-tuple-element.10), kind=kLoop, calls=%fused_computation | loop fusion | flops 5242880 | bytes 20971520 | tf_op jit(solution)/shard_map/stack | solution.py:161
  157.1 75.3 %all-gather.2.cloned.1.call-done = bf16[2,512,2560]{2,1,0:T(8,128)(2,1)} async-done(((bf16[2,128,2560]{2,1,0:T(8,128)(2,1)}), bf16[2,512,2560]{2,1,0:T(8,128)(2,1)}) %all-gather.2.cloned.1.call-update) | async-done | bytes 5242896 | tf_op jit(solution)/shard_map/all_gather | solution.py:159
  232.4 16.7 %convolution_convert_fusion = bf16[1024,2048]{1,0:T(8,128)(2,1)} fusion(bf16[1024,2560]{1,0:T(8,128)(2,1)} %bitcast.50, bf16[2048,2560]{1,0:T(8,128)(2,1)} %bitcast.43), kind=kOutput, calls=%fused_computation.4 | convolution fusion | flops 10739515392 | bytes 19922944 | tf_op jit(solution)/shard_map/dot_general | solution.py:16
  249.1 7.8 %reshape.25 = bf16[2,512,2,1024]{3,2,1,0:T(2,128)(2,1)} reshape(bf16[1024,2048]{1,0:T(8,128)(2,1)} %convolution_convert_fusion) | data formatting | bytes 8388608 | tf_op jit(solution)/shard_map/reshape | solution.py:168
  256.9 10.9 %constant_dynamic-slice_fusion.3 = (bf16[1,512,1,1024]{3,2,1,0:T(2,128)(2,1)S(1)}, bf16[1,512,1,1024]{3,2,1,0:T(2,128)(2,1)S(1)}, bf16[1,512,1,1024]{3,2,1,0:T(2,128)(2,1)S(1)}, bf16[1,512,1,1024]{3,2,1,0:T(2,128)(2,1)S(1)}) fusion(bf16[2,512,2,1024]{3,2,1,0:T(2,128)(2,1)} %reshape.25, s32[]{:T(128)S(6)} %select_n.130, s32[]{:T(128)S(6)} %select_n.132, ...), kind=kLoop, calls=%fused_computation.32 | loop fusion | bytes 8388628 | tf_op jit(solution)/shard_map/dynamic_slice | solution.py:172
  268.2 1.5 collective-permute-start.7
  271.0 1.5 collective-permute-start.8
  274.6 66.0 %psum.7 = f32[32]{0:T(128)S(1)} all-reduce(f32[32]{0:T(128)S(1)} %reshape.26), channel_id=1, replica_groups=mesh['ctx'=4,'head'=2,'rep'=4] {'ctx','rep'}, use_global_device_ids=true, to_apply=%region_2.3 | all-reduce | flops 32 | bytes 256 | tf_op jit(solution)/shard_map/psum | solution.py:147
  341.2 3.9 %fusion.3 = bf16[1,512,1024]{2,1,0:T(8,128)(2,1)} fusion(bf16[512,1024]{1,0:T(8,128)(2,1)} %collective-permute-done.9, bf16[512,1024]{1,0:T(8,128)(2,1)} %collective-permute-done.8, bf16[512,1024]{1,0:T(8,128)(2,1)} %collective-permute-done.7, bf16[1,512,1,1024]{3,2,1,0:T(2,128)(2,1)S(1)} %get-tuple-element.14), kind=kLoop, calls=%fused_computation.14 | loop fusion | flops 4194304 | bytes 5242880 | tf_op jit(solution)/shard_map/broadcast_in_dim | solution.py:186
  (60 shorter events, 12.8 us)
Async XLA Ops:
  7.2 225.3 %all-gather.2.cloned.1.call-start = ((), (), s32[]{:S(2)}) async-start(), calls=%async_computation | async-start | bytes 6553600 | tf_op jit(solution)/shard_map/all_gather | solution.py:159
  8.9 17.6 %collective-permute-start = (bf16[128,1024]{1,0:T(8,128)(2,1)}, bf16[128,1024]{1,0:T(8,128)(2,1)}, u32[]{:S(2)}, u32[]{:S(2)}) collective-permute-start(bf16[128,1024]{1,0:T(8,128)(2,1)} %pad_maximum_fusion.7), channel_id=1, source_target_pairs={{0,16},{8,24},{1,17},{9,25},{2,18},{10,26},{3,19},{11,27},{4,20},{... | collective-permute-start | bytes 786440 | tf_op jit(solution)/shard_map/ppermute | solution.py:90
  15.5 11.0 %collective-permute-start.1 = (bf16[128,1024]{1,0:T(8,128)(2,1)}, bf16[128,1024]{1,0:T(8,128)(2,1)}, u32[]{:S(2)}, u32[]{:S(2)}) collective-permute-start(bf16[128,1024]{1,0:T(8,128)(2,1)} %pad_maximum_fusion.7), channel_id=1, source_target_pairs={{0,8},{8,16},{16,24},{1,9},{9,17},{17,25},{2,10},{10,18},{18,26},{... | collective-permute-start | bytes 786440 | tf_op jit(solution)/shard_map/ppermute | solution.py:90
  20.5 5.0 %copy-start.7 = (bf16[512,512]{1,0:T(8,128)(2,1)S(1)}, bf16[512,512]{1,0:T(8,128)(2,1)}, u32[]{:S(2)}) copy-start(bf16[512,512]{1,0:T(8,128)(2,1)} %param.19) | copy-start | bytes 1572868
  20.5 5.0 %copy-start.8 = (bf16[512,512]{1,0:T(8,128)(2,1)S(1)}, bf16[512,512]{1,0:T(8,128)(2,1)}, u32[]{:S(2)}) copy-start(bf16[512,512]{1,0:T(8,128)(2,1)} %param.18) | copy-start | bytes 1572868
  20.5 5.8 %copy-start.9 = (s32[8]{0:T(128)S(1)}, s32[8]{0:T(128)}, u32[]{:S(2)}) copy-start(s32[8]{0:T(128)} %param.16) | copy-start | bytes 100
  20.5 6.0 %copy-start.10 = (f32[32]{0:T(128)S(1)}, f32[32]{0:T(128)}, u32[]{:S(2)}) copy-start(f32[32]{0:T(128)} %param.15) | copy-start | bytes 388
  20.5 6.0 %copy-start.5 = (bf16[1,128,512]{2,1,0:T(8,128)(2,1)S(1)}, bf16[1,128,512]{2,1,0:T(8,128)(2,1)}, u32[]{:S(2)}) copy-start(bf16[1,128,512]{2,1,0:T(8,128)(2,1)} %param.12) | copy-start | bytes 393220
  20.5 6.0 %copy-start.6 = (bf16[1,128,512]{2,1,0:T(8,128)(2,1)S(1)}, bf16[1,128,512]{2,1,0:T(8,128)(2,1)}, u32[]{:S(2)}) copy-start(bf16[1,128,512]{2,1,0:T(8,128)(2,1)} %param.11) | copy-start | bytes 393220
  25.5 2.3 copy-start
  25.5 2.3 copy-start.1
  47.1 3.1 copy-start.3
  47.2 15.4 %collective-permute-start.2 = (bf16[128,1024]{1,0:T(8,128)(2,1)S(1)}, bf16[128,1024]{1,0:T(8,128)(2,1)S(1)}, u32[]{:S(2)}, u32[]{:S(2)}) collective-permute-start(bf16[128,1024]{1,0:T(8,128)(2,1)S(1)} %get-tuple-element.24), channel_id=1, source_target_pairs={{8,0},{16,8},{24,16},{9,1},{17,9},{25,17},{10,2},{18,10},{26,18},{... | collective-permute-start | bytes 786440 | tf_op jit(solution)/shard_map/ppermute | solution.py:90
  48.7 27.2 %collective-permute-start.3 = (bf16[128,1024]{1,0:T(8,128)(2,1)S(1)}, bf16[128,1024]{1,0:T(8,128)(2,1)S(1)}, u32[]{:S(2)}, u32[]{:S(2)}) collective-permute-start(bf16[128,1024]{1,0:T(8,128)(2,1)S(1)} %get-tuple-element.25), channel_id=1, source_target_pairs={{16,0},{24,8},{17,1},{25,9},{18,2},{26,10},{19,3},{27,11},{20,4},{... | collective-permute-start | bytes 786440 | tf_op jit(solution)/shard_map/ppermute | solution.py:90
  50.4 74.8 %collective-permute-start.5 = (bf16[512,2560]{1,0:T(8,128)(2,1)S(1)}, bf16[512,2560]{1,0:T(8,128)(2,1)}, u32[]{:S(2)}, u32[]{:S(2)}) collective-permute-start(bf16[512,2560]{1,0:T(8,128)(2,1)S(1)} %pad_maximum_fusion.3), channel_id=1, source_target_pairs={{0,2},{1,3},{2,0},{3,1},{4,6},{5,7},{6,4},{7,5},{8,10},{9,11},{10,... | collective-permute-start | bytes 7864328 | tf_op jit(solution)/shard_map/ppermute | solution.py:94
  76.9 45.7 %collective-permute-start.4 = (bf16[128,2560]{1,0:T(8,128)(2,1)}, bf16[128,2560]{1,0:T(8,128)(2,1)}, u32[]{:S(2)}, u32[]{:S(2)}) collective-permute-start(bf16[128,2560]{1,0:T(8,128)(2,1)} %pad_maximum_fusion.6), channel_id=1, source_target_pairs={{0,2},{1,3},{2,0},{3,1},{4,6},{5,7},{6,4},{7,5},{8,10},{9,11},{10,... | collective-permute-start | bytes 1966088 | tf_op jit(solution)/shard_map/ppermute | solution.py:94
  123.9 1.2 copy-start.4
  128.0 3.0 copy-start.2
  131.0 9.0 %collective-permute-start.6 = (bf16[2,512,2560]{2,1,0:T(8,128)(2,1)}, bf16[2,512,2560]{2,1,0:T(8,128)(2,1)}, u32[]{:S(2)}, u32[]{:S(2)}) collective-permute-start(bf16[2,512,2560]{2,1,0:T(8,128)(2,1)} %pad_maximum_fusion.1), channel_id=1, source_target_pairs={{0,1},{1,0},{2,3},{3,2},{4,5},{5,4},{6,7},{7,6},{8,9},{9,8},{10,11... | collective-permute-start | bytes 15728648 | tf_op jit(solution)/shard_map/ppermute | solution.py:94
  268.2 73.0 %collective-permute-start.7 = (bf16[512,1024]{1,0:T(8,128)(2,1)S(1)}, bf16[512,1024]{1,0:T(8,128)(2,1)}, u32[]{:S(2)}, u32[]{:S(2)}) collective-permute-start(bf16[512,1024]{1,0:T(8,128)(2,1)S(1)} %bitcast.44), channel_id=1, source_target_pairs={{0,4},{1,5},{2,6},{3,7},{4,0},{5,1},{6,2},{7,3},{8,12},{9,13},{10,... | collective-permute-start | bytes 3145736 | tf_op jit(solution)/shard_map/ppermute | solution.py:185
  271.0 70.1 %collective-permute-start.8 = (bf16[512,1024]{1,0:T(8,128)(2,1)}, bf16[512,1024]{1,0:T(8,128)(2,1)}, u32[]{:S(2)}, u32[]{:S(2)}) collective-permute-start(bf16[512,1024]{1,0:T(8,128)(2,1)} %bitcast.39), channel_id=1, source_target_pairs={{0,2},{1,3},{2,0},{3,1},{4,6},{5,7},{6,4},{7,5},{8,10},{9,11},{10,... | collective-permute-start | bytes 3145736 | tf_op jit(solution)/shard_map/ppermute | solution.py:185
  273.9 67.3 %collective-permute-start.9 = (bf16[512,1024]{1,0:T(8,128)(2,1)}, bf16[512,1024]{1,0:T(8,128)(2,1)}, u32[]{:S(2)}, u32[]{:S(2)}) collective-permute-start(bf16[512,1024]{1,0:T(8,128)(2,1)} %bitcast.38), channel_id=1, source_target_pairs={{0,6},{1,7},{2,4},{3,5},{4,2},{5,3},{6,0},{7,1},{8,14},{9,15},{10,... | collective-permute-start | bytes 3145736 | tf_op jit(solution)/shard_map/ppermute | solution.py:185
Sparse Core Ops, SparseCore 0:
  125.3 107.1 all-gather.1

commit v2 on v1

--- a/solution.py
+++ b/solution.py
@@ -84,6 +84,187 @@
     )(scale, query, grad, key, value, row_seg, key_seg)
 
 
+def project_kernel(
+    mine_ref, other_ref, w0_ref, w1_ref, w2_ref, out_ref,
+    tokens, weights, sending, landing, own, local_sem, unit_send, unit_recv, part_send, part_recv,
+):
+    count, rows = tokens.shape[0], tokens.shape[2]
+    width = weights.shape[2]
+    mesh_id = pl.DeviceIdType.MESH
+    z, x, rep = lax.axis_index("ctx"), lax.axis_index("head"), lax.axis_index("rep")
+    y, k = rep // 2, rep % 2
+    peers = [
+        {"head": 1 - x},
+        {"rep": (1 - y) * 2 + k},
+        {"head": 1 - x, "rep": (1 - y) * 2 + k},
+        {"rep": y * 2 + 1 - k},
+    ]
+    has_left, has_right = z > 0, z < count - 1
+
+    local = [pltpu.make_async_copy(mine_ref, tokens.at[z, y], local_sem.at[0])]
+    places = ((y, k), (1 - y, k), (y, 1 - k))
+    for i, (ref, (high, low)) in enumerate(zip((w0_ref, w1_ref, w2_ref), places)):
+        local.append(pltpu.make_async_copy(ref, weights.at[high, low], local_sem.at[1 + i]))
+    for copy in local:
+        copy.start()
+
+    barrier = pltpu.get_barrier_semaphore()
+    for peer in peers:
+        pl.semaphore_signal(barrier, inc=1, device_id=peer, device_id_type=mesh_id)
+
+    @pl.when(has_left)
+    def _():
+        pl.semaphore_signal(barrier, inc=1, device_id={"ctx": z - 1}, device_id_type=mesh_id)
+
+    @pl.when(has_right)
+    def _():
+        pl.semaphore_signal(barrier, inc=1, device_id={"ctx": z + 1}, device_id_type=mesh_id)
+
+    pl.semaphore_wait(barrier, 4 + jnp.minimum(z, 1) + jnp.minimum(count - 1 - z, 1))
+
+    def across():
+        return pltpu.make_async_remote_copy(
+            src_ref=other_ref, dst_ref=tokens.at[z, y], send_sem=local_sem.at[5],
+            recv_sem=unit_recv.at[z, y], device_id=peers[1], device_id_type=mesh_id,
+        )
+
+    def along(b, p, side):
+        return pltpu.make_async_remote_copy(
+            src_ref=tokens.at[b, p], dst_ref=tokens.at[b, p], send_sem=unit_send.at[side, b, p],
+            recv_sem=unit_recv.at[b, p], device_id={"ctx": z + (2 * side - 1)},
+            device_id_type=mesh_id,
+        )
+
+    def part(kind, b):
+        return pltpu.make_async_remote_copy(
+            src_ref=sending.at[kind - 1, b], dst_ref=landing.at[kind - 1, b],
+            send_sem=part_send.at[kind - 1, b], recv_sem=part_recv.at[kind - 1, b],
+            device_id=peers[kind - 1], device_id_type=mesh_id,
+        )
+
+    def beside(low):
+        return pltpu.make_async_remote_copy(
+            src_ref=w1_ref, dst_ref=weights.at[1 - y, low], send_sem=local_sem.at[4],
+            recv_sem=local_sem.at[6], device_id=peers[3], device_id_type=mesh_id,
+        )
+
+    across().start()
+    beside(k).start()
+    local[0].wait()
+
+    def product(b, p, dx, low):
+        high = x if dx == 0 else 1 - x
+        return contract(tokens[b, p], weights[high, low], 1, 1)
+
+    def visit(t, carried):
+        step, second, side = t // 4, (t // 2) % 2, t % 2
+        b = z + step * (2 * side - 1)
+        p = y + second * (1 - 2 * y)
+        valid = (b >= 0) & (b < count) & ((step > 0) | (side == 0))
+
+        @pl.when(valid)
+        def _():
+            @pl.when((step > 0) | (second == 1))
+            def _():
+                along(b, p, 0).wait_recv()
+
+            @pl.when(has_left & ((side == 1) | (step == 0)))
+            def _():
+                along(b, p, 0).start()
+
+            @pl.when(has_right & (side == 0))
+            def _():
+                along(b, p, 1).start()
+
+            @pl.when(t == 0)
+            def _():
+                for copy in local[1:]:
+                    copy.wait()
+                beside(1 - k).wait_recv()
+
+            for low in range(2):
+                sending[second * 2, b, :, low * width : (low + 1) * width] = product(
+                    b, p, 1, low
+                ).astype(jnp.bfloat16)
+
+            for low in range(2):
+                value = product(b, p, 0, low)
+
+                @pl.when(second == 0)
+                def _():
+                    own[b, :, low * width : (low + 1) * width] = value
+
+                @pl.when(second == 1)
+                def _():
+                    sending[1, b, :, low * width : (low + 1) * width] = value.astype(jnp.bfloat16)
+
+            @pl.when(second == 0)
+            def _():
+                part(1, b).start()
+
+            @pl.when(second == 1)
+            def _():
+                part(3, b).start()
+                part(2, b).start()
+
+        return carried
+
+    lax.fori_loop(0, 4 * count, visit, 0)
+
+    def finish(b, carried):
+        for kind in (1, 2, 3):
+            part(kind, b).wait()
+        total = own[b]
+        for kind in (1, 2, 3):
+            total = total + landing[kind - 1, b].astype(jnp.float32)
+        out_ref[pl.ds(pl.multiple_of(b * rows, rows), rows), :] = total.astype(jnp.bfloat16)
+        for second in range(2):
+
+            @pl.when(has_left & (b >= z))
+            def _():
+                along(b, second, 0).wait_send()
+
+            @pl.when(has_right & (b <= z))
+            def _():
+                along(b, second, 1).wait_send()
+
+        return carried
+
+    lax.fori_loop(0, count, finish, 0)
+    across().wait_send()
+    beside(k).wait_send()
+
+
+def project(mine, other, weights, count):
+    rows, depth = mine.shape
+    width = weights[0].shape[0]
+    bf16 = jnp.bfloat16
+    dma = pltpu.SemaphoreType.DMA
+    vmem = pl.BlockSpec(memory_space=pltpu.VMEM)
+    return pl.pallas_call(
+        project_kernel,
+        in_specs=[vmem, vmem] + [pl.BlockSpec(memory_space=pl.ANY)] * 3,
+        out_specs=vmem,
+        out_shape=jax.ShapeDtypeStruct((count * rows, 2 * width), bf16),
+        scratch_shapes=[
+            pltpu.VMEM((count, 2, rows, depth), bf16),
+            pltpu.VMEM((2, 2, width, depth), bf16),
+            pltpu.VMEM((3, count, rows, 2 * width), bf16),
+            pltpu.VMEM((3, count, rows, 2 * width), bf16),
+            pltpu.VMEM((count, rows, 2 * width), jnp.float32),
+            dma((7,)), dma((2, count, 2)), dma((count, 2)), dma((3, count)), dma((3, count)),
+        ],
+        compiler_params=pltpu.CompilerParams(
+            collective_id=0, has_side_effects=True, vmem_limit_bytes=50 * 1024 * 1024
+        ),
+        cost_estimate=pl.CostEstimate(
+            flops=2 * count * 2 * rows * depth * 4 * width,
+            bytes_accessed=2 * 4 * width * depth, transcendentals=0,
+        ),
+        name="project",
+    )(mine, other, *weights)
+
+
 def moved(block, distance):
     count = lax.axis_size("ctx")
     route = [(i, i + distance) for i in range(count) if 0 <= i + distance < count]
@@ -133,8 +314,7 @@
     weights = (w_query, w_key, w_value)
     weight_mine = half_columns(weights, high)
     weight_other = swapped(half_columns(weights, 1 - high), 2)
-    weight_pair = in_order(weight_mine, weight_other, high)
-    weight_far = swapped(weight_pair, 1)
+    far_mine = swapped(weight_mine, 1)
 
     head_ids = lax.axis_index("head") * local_heads + jnp.arange(local_heads, dtype=jnp.int32)
     ablate = jnp.any(head_ids[:, None] == ablated_heads[None, :], axis=1)
@@ -154,7 +334,15 @@
     total = total.astype(jnp.bfloat16)
     grads = (dq, total[:, :narrow], total[:, narrow:])
     grad_mine = half_columns(grads, high)
-    grad_other = swapped(half_columns(grads, 1 - high), 2)
+    grad_other = half_columns(grads, 1 - high)
+    if lax.axis_size("head") == 2 and rep_count == 4:
+        pieces = (weight_mine, weight_other, far_mine)
+        result = project(grad_mine, grad_other, pieces, block_count)
+        return (result[None], mask_grad)
+
+    grad_other = swapped(grad_other, 2)
+    weight_pair = in_order(weight_mine, weight_other, high)
+    weight_far = in_order(far_mine, swapped(weight_other, 1), high)
     grad_pair = in_order(grad_mine, grad_other, high)
     tokens = lax.all_gather(grad_pair, "ctx", axis=1, tiled=True)
     tokens = tokens.reshape(2 * seq_len, -1)

time: 352 us -> 197 us (0.56)
  waiting for transfers between devices: 152 us -> 0.02 us
  Pallas kernels: 19.4 us -> 117 us
  other arithmetic: 33.9 us -> 6.54 us
  local copies, waits for them, and re-layouts: 28.8 us -> 4.27 us
  matrix products: 16.7 us -> 0 us
  between operations: 14.3 us -> 0.91 us
  blocking collectives: 66 us -> 53.4 us
  starting transfers between devices: 20.4 us -> 14.3 us
    pallas_call x0 -> x1, Pallas kernels: none -> 97.9 us  [project(): pl.pallas_call(project_kernel, in_specs=[vmem, vmem] + [pl.BlockSpec(memo...]
    all_gather x1 -> x0, waiting for transfers between devices: 75.3 us -> none  [on_device(): tokens = lax.all_gather(grad_pair, 'ctx', axis=1, tiled=True)]
    ppermute x3 -> x2, waiting for transfers between devices: 53.2 us -> 0.01 us  [swapped(): lax.ppermute(block, 'rep', [(i, i ^ flip) for i in range(lax.axis_size('r...]
    another operation x6 -> x0, other arithmetic: 25.3 us -> none  [the longest x2 17 us: on_device(): jnp.stack([jnp.where(low == 0, weight_pair, weight_far), jnp.where(low ==...]
    ppermute x4, waiting for transfers between devices: 23.8 us -> 0.01 us  [moved(): return lax.ppermute(block, 'ctx', route)]
    dot_general x1 -> x0, matrix products: 16.7 us -> none  [contract(): lax.dot_general(left, right, (((left_dim,), (right_dim,)), ((), ())), pre...]
    psum x1, blocking collectives: 66 us -> 53.4 us  [on_device(): lax.psum(mask_terms, ('ctx', 'rep')) / math.sqrt(rep_count * seq_len)]
    dynamic_slice x1 -> x0, local copies, waits for them, and re-layouts: 10.9 us -> none  [piece_for(): return lax.dynamic_slice_in_dim(taken, column, 1, 2)[0, :, 0]]
  transfers between devices with their start and end apart: 11 -> 6, of which waited for: 5 -> 0; matrix products, arithmetic and copies ran while one was open for 10% -> 4% of each run, Pallas kernels for 0% -> 10%
where the time goes in v2:
time: 197 us
  Pallas kernels  117 us (59%)
  blocking collectives  53.4 us (27%)
  starting transfers between devices  14.3 us (7%)
  other arithmetic  6.54 us (3%)
  local copies, waits for them, and re-layouts  4.27 us (2%)
    pallas_call x1, Pallas kernels, project(): pl.pallas_call(project_kernel, in_specs=[vmem, vmem] + [pl.BlockSpec(memo...  97.9 us
    psum x1, blocking collectives, on_device(): lax.psum(mask_terms, ('ctx', 'rep')) / math.sqrt(rep_count * seq_len)  53.4 us
    pallas_call x1, Pallas kernels, attention(): pl.pallas_call(functools.partial(attention_kernel, per_group), grid=(grou...  19.4 us
    ppermute x4, starting transfers between devices, moved(): return lax.ppermute(block, 'ctx', route)  12.7 us
  transfers between devices with their start and end apart: 6, of which 0 were waited for; matrix products, arithmetic and copies ran while one was open for 4% of the time, Pallas kernels for 10%

profile of v2, /device:TPU:0, one launch (start us, length us, event | category | flops | bytes accessed | tf_op | source)
XLA Modules:
  0.0 196.6 jit_solution(10933484291401169874)
XLA Ops:
  0.6 1.0 pad_maximum_fusion.4
  1.6 4.9 %collective-permute-start.1 = (bf16[128,1024]{1,0:T(8,128)(2,1)S(1)}, bf16[128,1024]{1,0:T(8,128)(2,1)S(1)}, u32[]{:S(2)}, u32[]{:S(2)}) collective-permute-start(bf16[128,1024]{1,0:T(8,128)(2,1)S(1)} %pad_maximum_fusion.4), channel_id=1, source_target_pairs={{0,8},{8,16},{16,24},{1,9},{9,17},{17,25},{2,10},{10,18},{18,26},{... | collective-permute-start | bytes 786440 | tf_op jit(solution)/shard_map/ppermute | solution.py:271
  6.6 5.2 %collective-permute-start = (bf16[128,1024]{1,0:T(8,128)(2,1)S(1)}, bf16[128,1024]{1,0:T(8,128)(2,1)}, u32[]{:S(2)}, u32[]{:S(2)}) collective-permute-start(bf16[128,1024]{1,0:T(8,128)(2,1)S(1)} %pad_maximum_fusion.4), channel_id=1, source_target_pairs={{0,16},{8,24},{1,17},{9,25},{2,18},{10,26},{3,19},{11,27},{4,20},{... | collective-permute-start | bytes 786440 | tf_op jit(solution)/shard_map/ppermute | solution.py:271
  11.8 2.6 %constant_dynamic-slice_fusion.2 = (bf16[512,2048]{1,0:T(8,128)(2,1)S(1)}, bf16[512,2048]{1,0:T(8,128)(2,1)S(1)}) fusion(bf16[512,4096]{1,0:T(8,128)(2,1)} %param.17, s32[]{:T(128)S(6)} %select_n.37, s32[]{:T(128)S(6)} %select_n.35), kind=kLoop, calls=%fused_computation.13 | loop fusion | bytes 8388616 | tf_op jit(solution)/shard_map/dynamic_slice | solution.py:282
  14.4 0.1 constant_dynamic-slice_fusion
  14.5 1.7 pad_maximum_fusion.1
  16.2 1.5 collective-permute-start.4
  17.8 1.7 pad_maximum_fusion.w0_ref
  19.5 0.1 pad_dynamic-slice_fusion
  19.6 0.1 compare_reduce_fusion
  19.7 0.1 copy.13.row_seg_ref
  19.9 1.2 maximum_maximum_fusion
  21.1 0.1 fusion.1
  21.2 19.4 %attention.1 = (bf16[128,4096]{1,0:T(8,128)(2,1)S(1)}, bf16[384,512]{1,0:T(8,128)(2,1)S(1)}, bf16[384,512]{1,0:T(8,128)(2,1)S(1)}, f32[4,8,128]{2,1,0:T(8,128)S(1)}) custom-call(f32[32]{0:T(128)S(1)} %broadcast_select_fusion.scale_ref, bf16[128,4096]{1,0:T(8,128)(2,1)S(1)} %bitcast.9, bf16[128,4096]{1,0:T(8,128)(2,1)S(1)} %bitcast.10, ...), custom_call_target="tpu_custom_call" | custom-call | flops 2415919104 | bytes 3145728 | tf_op jit(solution)/shard_map/attention/pallas_call | solution.py:64
  40.7 1.3 collective-permute-start.3
  42.0 1.3 collective-permute-start.2
  43.3 0.1 reduce_sum.9
  43.4 0.1 reshape.12
  43.5 53.4 %psum.7 = f32[32]{0:T(128)S(1)} all-reduce(f32[32]{0:T(128)S(1)} %reshape.12), channel_id=1, replica_groups=mesh['ctx'=4,'head'=2,'rep'=4] {'ctx','rep'}, use_global_device_ids=true, to_apply=%region_2.3 | all-reduce | flops 32 | bytes 256 | tf_op jit(solution)/shard_map/psum | solution.py:327
  96.8 0.5 broadcast_multiply_fusion
  97.4 0.1 constant_dynamic-slice_fusion.8
  97.5 0.1 add_convert_fusion
  97.8 97.9 %project.1 = bf16[512,1024]{1,0:T(8,128)(2,1)S(1)} custom-call(bf16[128,2560]{1,0:T(8,128)(2,1)S(1)} %pad_maximum_fusion.2.mine_ref, bf16[128,2560]{1,0:T(8,128)(2,1)S(1)} %pad_maximum_fusion.3.other_ref, bf16[512,2560]{1,0:T(8,128)(2,1)} %pad_maximum_fusion.w0_ref, bf16[512,2560]{1,0:T(8,128)(2,1)} %collective-permute-done.4.w1_ref, ...), custom_call_target="tpu_custom_call" | custom-call | flops 10737418240 | bytes 10485760 | tf_op jit(solution)/shard_map/project/pallas_call | solution.py:244
  195.6 1.0 copy.16
  (36 shorter events, 0.3 us)
Async XLA Ops:
  1.6 18.2 %collective-permute-start.1 = (bf16[128,1024]{1,0:T(8,128)(2,1)S(1)}, bf16[128,1024]{1,0:T(8,128)(2,1)S(1)}, u32[]{:S(2)}, u32[]{:S(2)}) collective-permute-start(bf16[128,1024]{1,0:T(8,128)(2,1)S(1)} %pad_maximum_fusion.4), channel_id=1, source_target_pairs={{0,8},{8,16},{16,24},{1,9},{9,17},{17,25},{2,10},{10,18},{18,26},{... | collective-permute-start | bytes 786440 | tf_op jit(solution)/shard_map/ppermute | solution.py:271
  6.6 13.3 %collective-permute-start = (bf16[128,1024]{1,0:T(8,128)(2,1)S(1)}, bf16[128,1024]{1,0:T(8,128)(2,1)}, u32[]{:S(2)}, u32[]{:S(2)}) collective-permute-start(bf16[128,1024]{1,0:T(8,128)(2,1)S(1)} %pad_maximum_fusion.4), channel_id=1, source_target_pairs={{0,16},{8,24},{1,17},{9,25},{2,18},{10,26},{3,19},{11,27},{4,20},{... | collective-permute-start | bytes 786440 | tf_op jit(solution)/shard_map/ppermute | solution.py:271
  11.8 2.6 %copy-start.4 = (bf16[512,512]{1,0:T(8,128)(2,1)S(1)}, bf16[512,512]{1,0:T(8,128)(2,1)}, u32[]{:S(2)}) copy-start(bf16[512,512]{1,0:T(8,128)(2,1)} %param.19) | copy-start | bytes 1572868
  11.8 2.6 %copy-start.5 = (bf16[512,512]{1,0:T(8,128)(2,1)S(1)}, bf16[512,512]{1,0:T(8,128)(2,1)}, u32[]{:S(2)}) copy-start(bf16[512,512]{1,0:T(8,128)(2,1)} %param.18) | copy-start | bytes 1572868
  16.2 81.5 %collective-permute-start.4 = (bf16[512,2560]{1,0:T(8,128)(2,1)}, bf16[512,2560]{1,0:T(8,128)(2,1)}, u32[]{:S(2)}, u32[]{:S(2)}) collective-permute-start(bf16[512,2560]{1,0:T(8,128)(2,1)} %pad_maximum_fusion.1), channel_id=1, source_target_pairs={{0,2},{1,3},{2,0},{3,1},{4,6},{5,7},{6,4},{7,5},{8,10},{9,11},{10,... | collective-permute-start | bytes 7864328 | tf_op jit(solution)/shard_map/ppermute | solution.py:275
  17.8 1.7 copy-start.6
  17.8 1.8 copy-start.7
  17.8 2.1 %copy-start.8 = (f32[32]{0:T(128)S(1)}, f32[32]{0:T(128)}, u32[]{:S(2)}) copy-start(f32[32]{0:T(128)} %param.15) | copy-start | bytes 388
  17.8 2.1 %copy-start.2 = (bf16[1,128,512]{2,1,0:T(8,128)(2,1)S(1)}, bf16[1,128,512]{2,1,0:T(8,128)(2,1)}, u32[]{:S(2)}) copy-start(bf16[1,128,512]{2,1,0:T(8,128)(2,1)} %param.12) | copy-start | bytes 393220
  17.8 2.1 %copy-start.3 = (bf16[1,128,512]{2,1,0:T(8,128)(2,1)S(1)}, bf16[1,128,512]{2,1,0:T(8,128)(2,1)}, u32[]{:S(2)}) copy-start(bf16[1,128,512]{2,1,0:T(8,128)(2,1)} %param.11) | copy-start | bytes 393220
  19.5 1.7 copy-start
  19.5 1.7 copy-start.1
  19.5 78.3 %collective-permute-start.5 = (bf16[512,2560]{1,0:T(8,128)(2,1)}, bf16[512,2560]{1,0:T(8,128)(2,1)}, u32[]{:S(2)}, u32[]{:S(2)}) collective-permute-start(bf16[512,2560]{1,0:T(8,128)(2,1)} %pad_maximum_fusion.w0_ref), channel_id=1, source_target_pairs={{0,1},{1,0},{2,3},{3,2},{4,5},{5,4},{6,7},{7,6},{8,9},{9,8},{10,11... | collective-permute-start | bytes 7864328 | tf_op jit(solution)/shard_map/ppermute | solution.py:275
  40.7 56.8 %collective-permute-start.3 = (bf16[128,1024]{1,0:T(8,128)(2,1)S(1)}, bf16[128,1024]{1,0:T(8,128)(2,1)S(1)}, u32[]{:S(2)}, u32[]{:S(2)}) collective-permute-start(bf16[128,1024]{1,0:T(8,128)(2,1)S(1)} %get-tuple-element.15), channel_id=1, source_target_pairs={{16,0},{24,8},{17,1},{25,9},{18,2},{26,10},{19,3},{27,11},{20,4},{... | collective-permute-start | bytes 786440 | tf_op jit(solution)/shard_map/ppermute | solution.py:271
  42.0 55.5 %collective-permute-start.2 = (bf16[128,1024]{1,0:T(8,128)(2,1)S(1)}, bf16[128,1024]{1,0:T(8,128)(2,1)S(1)}, u32[]{:S(2)}, u32[]{:S(2)}) collective-permute-start(bf16[128,1024]{1,0:T(8,128)(2,1)S(1)} %get-tuple-element.14), channel_id=1, source_target_pairs={{8,0},{16,8},{24,16},{9,1},{17,9},{25,17},{10,2},{18,10},{26,18},{... | collective-permute-start | bytes 786440 | tf_op jit(solution)/shard_map/ppermute | solution.py:271

commit v3 on v2

--- a/solution.py
+++ b/solution.py
@@ -85,11 +85,13 @@
 
 
 def project_kernel(
-    mine_ref, other_ref, w0_ref, w1_ref, w2_ref, out_ref,
-    tokens, weights, sending, landing, own, local_sem, unit_send, unit_recv, part_send, part_recv,
+    mine_ref, other_ref, term_ref, w0_ref, w1_ref, w2_ref, wx_ref, out_ref, mask_ref,
+    tokens, weights, sending, landing, own, terms, sums, local_sem, unit_send, unit_recv,
+    part_send, part_recv, term_send, term_recv,
 ):
     count, rows = tokens.shape[0], tokens.shape[2]
     width = weights.shape[2]
+    early = 8
     mesh_id = pl.DeviceIdType.MESH
     z, x, rep = lax.axis_index("ctx"), lax.axis_index("head"), lax.axis_index("rep")
     y, k = rep // 2, rep % 2
@@ -103,8 +105,10 @@
 
     local = [pltpu.make_async_copy(mine_ref, tokens.at[z, y], local_sem.at[0])]
     places = ((y, k), (1 - y, k), (y, 1 - k))
+    near = w1_ref.shape[0]
     for i, (ref, (high, low)) in enumerate(zip((w0_ref, w1_ref, w2_ref), places)):
-        local.append(pltpu.make_async_copy(ref, weights.at[high, low], local_sem.at[1 + i]))
+        filled = weights.at[high, low, pl.ds(0, ref.shape[0])]
+        local.append(pltpu.make_async_copy(ref, filled, local_sem.at[1 + i]))
     for copy in local:
         copy.start()
 
@@ -128,6 +132,40 @@
             recv_sem=unit_recv.at[z, y], device_id=peers[1], device_id_type=mesh_id,
         )
 
+    def across_term():
+        return pltpu.make_async_remote_copy(
+            src_ref=term_ref, dst_ref=terms.at[z, y], send_sem=local_sem.at[7],
+            recv_sem=term_recv.at[z, y], device_id=peers[1], device_id_type=mesh_id,
+        )
+
+    def along_term(b, p, side):
+        return pltpu.make_async_remote_copy(
+            src_ref=terms.at[b, p], dst_ref=terms.at[b, p], send_sem=term_send.at[side, b, p],
+            recv_sem=term_recv.at[b, p], device_id={"ctx": z + (2 * side - 1)},
+            device_id_type=mesh_id,
+        )
+
+    def beside_sum():
+        return pltpu.make_async_remote_copy(
+            src_ref=sums.at[0], dst_ref=sums.at[1], send_sem=local_sem.at[8],
+            recv_sem=local_sem.at[9], device_id=peers[3], device_id_type=mesh_id,
+        )
+
+    def rest_across(high):
+        return pltpu.make_async_remote_copy(
+            src_ref=wx_ref, dst_ref=weights.at[high, k, pl.ds(near, width - near)],
+            send_sem=local_sem.at[10], recv_sem=local_sem.at[11], device_id=peers[1],
+            device_id_type=mesh_id,
+        )
+
+    def rest_beside(low):
+        rest = pl.ds(near, width - near)
+        return pltpu.make_async_remote_copy(
+            src_ref=weights.at[1 - y, k, rest], dst_ref=weights.at[1 - y, low, rest],
+            send_sem=local_sem.at[12], recv_sem=local_sem.at[13], device_id=peers[3],
+            device_id_type=mesh_id,
+        )
+
     def along(b, p, side):
         return pltpu.make_async_remote_copy(
             src_ref=tokens.at[b, p], dst_ref=tokens.at[b, p], send_sem=unit_send.at[side, b, p],
@@ -144,11 +182,14 @@
 
     def beside(low):
         return pltpu.make_async_remote_copy(
-            src_ref=w1_ref, dst_ref=weights.at[1 - y, low], send_sem=local_sem.at[4],
+            src_ref=w1_ref, dst_ref=weights.at[1 - y, low, pl.ds(0, near)], send_sem=local_sem.at[4],
             recv_sem=local_sem.at[6], device_id=peers[3], device_id_type=mesh_id,
         )
 
+    terms[z, y] = term_ref[...]
+    across_term().start()
     across().start()
+    rest_across(y).start()
     beside(k).start()
     local[0].wait()
 
@@ -156,32 +197,53 @@
         high = x if dx == 0 else 1 - x
         return contract(tokens[b, p], weights[high, low], 1, 1)
 
-    def visit(t, carried):
+    def unit(t):
         step, second, side = t // 4, (t // 2) % 2, t % 2
         b = z + step * (2 * side - 1)
         p = y + second * (1 - 2 * y)
-        valid = (b >= 0) & (b < count) & ((step > 0) | (side == 0))
+        return step, second, side, b, p, (b >= 0) & (b < count) & ((step > 0) | (side == 0))
+
+    def receive(t, carried):
+        step, second, side, b, p, valid = unit(t)
 
         @pl.when(valid)
         def _():
             @pl.when((step > 0) | (second == 1))
             def _():
                 along(b, p, 0).wait_recv()
+                along_term(b, p, 0).wait_recv()
 
             @pl.when(has_left & ((side == 1) | (step == 0)))
             def _():
                 along(b, p, 0).start()
+                along_term(b, p, 0).start()
 
             @pl.when(has_right & (side == 0))
             def _():
                 along(b, p, 1).start()
-
-            @pl.when(t == 0)
-            def _():
-                for copy in local[1:]:
-                    copy.wait()
-                beside(1 - k).wait_recv()
-
+                along_term(b, p, 1).start()
+
+        return carried
+
+    def visit(t, carried):
+        step, second, side, b, p, valid = unit(t)
+
+        @pl.when(t == 0)
+        def _():
+            lax.fori_loop(0, early, receive, 0)
+            for copy in local[1:]:
+                copy.wait()
+            beside(1 - k).wait_recv()
+            rest_across(1 - y).wait_recv()
+            rest_beside(k).start()
+            rest_beside(1 - k).wait_recv()
+
+        @pl.when(t >= early)
+        def _():
+            receive(t, 0)
+
+        @pl.when(valid)
+        def _():
             for low in range(2):
                 sending[second * 2, b, :, low * width : (low + 1) * width] = product(
                     b, p, 1, low
@@ -210,6 +272,9 @@
         return carried
 
     lax.fori_loop(0, 4 * count, visit, 0)
+
+    sums[0] = sum(terms[b, p] for b in range(count) for p in range(2))
+    beside_sum().start()
 
     def finish(b, carried):
         for kind in (1, 2, 3):
@@ -223,19 +288,26 @@
             @pl.when(has_left & (b >= z))
             def _():
                 along(b, second, 0).wait_send()
+                along_term(b, second, 0).wait_send()
 
             @pl.when(has_right & (b <= z))
             def _():
                 along(b, second, 1).wait_send()
+                along_term(b, second, 1).wait_send()
 
         return carried
 
     lax.fori_loop(0, count, finish, 0)
+    beside_sum().wait()
+    mask_ref[...] = sums[0] + sums[1]
     across().wait_send()
+    across_term().wait_send()
     beside(k).wait_send()
-
-
-def project(mine, other, weights, count):
+    rest_across(y).wait_send()
+    rest_beside(k).wait_send()
+
+
+def project(mine, other, term, weights, count):
     rows, depth = mine.shape
     width = weights[0].shape[0]
     bf16 = jnp.bfloat16
@@ -243,16 +315,22 @@
     vmem = pl.BlockSpec(memory_space=pltpu.VMEM)
     return pl.pallas_call(
         project_kernel,
-        in_specs=[vmem, vmem] + [pl.BlockSpec(memory_space=pl.ANY)] * 3,
-        out_specs=vmem,
-        out_shape=jax.ShapeDtypeStruct((count * rows, 2 * width), bf16),
+        in_specs=[vmem] * 3 + [pl.BlockSpec(memory_space=pl.ANY)] * 4,
+        out_specs=[vmem, vmem],
+        out_shape=[
+            jax.ShapeDtypeStruct((count * rows, 2 * width), bf16),
+            jax.ShapeDtypeStruct(term.shape, jnp.float32),
+        ],
         scratch_shapes=[
             pltpu.VMEM((count, 2, rows, depth), bf16),
             pltpu.VMEM((2, 2, width, depth), bf16),
             pltpu.VMEM((3, count, rows, 2 * width), bf16),
             pltpu.VMEM((3, count, rows, 2 * width), bf16),
             pltpu.VMEM((count, rows, 2 * width), jnp.float32),
-            dma((7,)), dma((2, count, 2)), dma((count, 2)), dma((3, count)), dma((3, count)),
+            pltpu.VMEM((count, 2) + term.shape, jnp.float32),
+            pltpu.VMEM((2,) + term.shape, jnp.float32),
+            dma((14,)), dma((2, count, 2)), dma((count, 2)), dma((3, count)), dma((3, count)),
+            dma((2, count, 2)), dma((count, 2)),
         ],
         compiler_params=pltpu.CompilerParams(
             collective_id=0, has_side_effects=True, vmem_limit_bytes=50 * 1024 * 1024
@@ -262,7 +340,7 @@
             bytes_accessed=2 * 4 * width * depth, transcendentals=0,
         ),
         name="project",
-    )(mine, other, *weights)
+    )(mine, other, term, *weights)
 
 
 def moved(block, distance):
@@ -313,7 +391,10 @@
 
     weights = (w_query, w_key, w_value)
     weight_mine = half_columns(weights, high)
-    weight_other = swapped(half_columns(weights, 1 - high), 2)
+    fused = lax.axis_size("head") == 2 and rep_count == 4 and block_count > 1
+    weight_sent = half_columns(weights, 1 - high)
+    near = weight_sent.shape[0] * 3 // 4 if fused else weight_sent.shape[0]
+    weight_other = swapped(weight_sent[:near], 2)
     far_mine = swapped(weight_mine, 1)
 
     head_ids = lax.axis_index("head") * local_heads + jnp.arange(local_heads, dtype=jnp.int32)
@@ -324,7 +405,7 @@
         row_seg[:, None], key_seg[None, :],
     )
     mask_terms = jnp.sum(mask_rows, axis=2).reshape(local_heads)
-    mask_grad = lax.psum(mask_terms, ("ctx", "rep")) / math.sqrt(rep_count * seq_len)
+    mask_norm = math.sqrt(rep_count * seq_len)
 
     pair = jnp.concatenate([dk, dv], axis=1)
     total = pair[before * rows_dev :].astype(jnp.float32)
@@ -335,10 +416,13 @@
     grads = (dq, total[:, :narrow], total[:, narrow:])
     grad_mine = half_columns(grads, high)
     grad_other = half_columns(grads, 1 - high)
-    if lax.axis_size("head") == 2 and rep_count == 4:
-        pieces = (weight_mine, weight_other, far_mine)
-        result = project(grad_mine, grad_other, pieces, block_count)
-        return (result[None], mask_grad)
+    if fused:
+        pieces = (weight_mine, weight_other, far_mine, weight_sent[near:])
+        term = jnp.zeros((8, DH), jnp.float32).at[0, :local_heads].set(mask_terms)
+        result, mask_sum = project(grad_mine, grad_other, term, pieces, block_count)
+        return (result[None], mask_sum[0, :local_heads] / mask_norm)
+
+    mask_grad = lax.psum(mask_terms, ("ctx", "rep")) / mask_norm
 
     grad_other = swapped(grad_other, 2)
     weight_pair = in_order(weight_mine, weight_other, high)

time: 197 us -> 174 us (0.88)
  blocking collectives: 53.4 us -> 0 us
  waiting for transfers between devices: 0.02 us -> 21.1 us
  Pallas kernels: 117 us -> 124 us
  local copies, waits for them, and re-layouts: 4.27 us -> 9.57 us
    psum x1 -> x0, blocking collectives: 53.4 us -> none  [on_device(): lax.psum(mask_terms, ('ctx', 'rep')) / math.sqrt(rep_count * seq_len)]
    ppermute x4, waiting for transfers between devices: 0.01 us -> 21.1 us  [moved(): return lax.ppermute(block, 'ctx', route)]
    pallas_call x1, Pallas kernels: 97.9 us -> 104 us  [project(): pl.pallas_call(project_kernel, in_specs=[vmem] * 3 + [pl.BlockSpec(memory...]
    unnamed x20 -> x24, local copies, waits for them, and re-layouts: 1.04 us -> 4.04 us
  transfers between devices with their start and end apart: 6 -> 6, of which waited for: 0 -> 2; matrix products, arithmetic and copies ran while one was open for 4% -> 5% of each run, Pallas kernels for 10% -> 11%
where the time goes in v3:
time: 174 us
  Pallas kernels  124 us (71%)
  waiting for transfers between devices  21.1 us (12%)
  starting transfers between devices  13.5 us (8%)
  local copies, waits for them, and re-layouts  9.57 us (6%)
  other arithmetic  4.84 us (3%)
    pallas_call x1, Pallas kernels, project(): pl.pallas_call(project_kernel, in_specs=[vmem] * 3 + [pl.BlockSpec(memory...  104 us
    ppermute x4, waiting for transfers between devices, moved(): return lax.ppermute(block, 'ctx', route)  21.1 us
    pallas_call x1, Pallas kernels, attention(): pl.pallas_call(functools.partial(attention_kernel, per_group), grid=(grou...  19.3 us
    ppermute x4, starting transfers between devices, moved(): return lax.ppermute(block, 'ctx', route)  12 us
    unnamed x24, local copies, waits for them, and re-layouts  4.04 us
  transfers between devices with their start and end apart: 6, of which 2 were waited for; matrix products, arithmetic and copies ran while one was open for 5% of the time, Pallas kernels for 11%

profile of v3, /device:TPU:0, one launch (start us, length us, event | category | flops | bytes accessed | tf_op | source)
XLA Modules:
  0.0 173.6 jit_solution(1253141410501425165)
XLA Ops:
  0.6 1.0 pad_maximum_fusion.5
  1.6 4.9 %collective-permute-start.1 = (bf16[128,1024]{1,0:T(8,128)(2,1)S(1)}, bf16[128,1024]{1,0:T(8,128)(2,1)S(1)}, u32[]{:S(2)}, u32[]{:S(2)}) collective-permute-start(bf16[128,1024]{1,0:T(8,128)(2,1)S(1)} %pad_maximum_fusion.5), channel_id=1, source_target_pairs={{0,8},{8,16},{16,24},{1,9},{9,17},{17,25},{2,10},{10,18},{18,26},{... | collective-permute-start | bytes 786440 | tf_op jit(solution)/shard_map/ppermute | solution.py:349
  6.6 4.5 %collective-permute-start = (bf16[128,1024]{1,0:T(8,128)(2,1)S(1)}, bf16[128,1024]{1,0:T(8,128)(2,1)S(1)}, u32[]{:S(2)}, u32[]{:S(2)}) collective-permute-start(bf16[128,1024]{1,0:T(8,128)(2,1)S(1)} %pad_maximum_fusion.5), channel_id=1, source_target_pairs={{0,16},{8,24},{1,17},{9,25},{2,18},{10,26},{3,19},{11,27},{4,20},{... | collective-permute-start | bytes 786440 | tf_op jit(solution)/shard_map/ppermute | solution.py:349
  11.1 2.6 %constant_dynamic-slice_fusion.2 = (bf16[512,2048]{1,0:T(8,128)(2,1)S(1)}, bf16[512,2048]{1,0:T(8,128)(2,1)S(1)}) fusion(bf16[512,4096]{1,0:T(8,128)(2,1)} %param.19, s32[]{:T(128)S(6)} %select_n.37, s32[]{:T(128)S(6)} %select_n.35), kind=kLoop, calls=%fused_computation.14 | loop fusion | bytes 8388616 | tf_op jit(solution)/shard_map/dynamic_slice | solution.py:360
  13.9 0.2 pad_maximum_fusion.1
  14.1 1.0 copy-done.2
  15.1 1.5 slice.67
  16.6 1.5 collective-permute-start.4
  18.2 1.7 pad_maximum_fusion.w0_ref
  19.9 0.1 pad_dynamic-slice_fusion
  20.0 0.1 compare_reduce_fusion
  20.1 0.1 copy.13.row_seg_ref
  20.4 0.7 copy-done
  21.1 1.2 copy-done.1
  22.3 19.3 %attention.1 = (bf16[128,4096]{1,0:T(8,128)(2,1)S(1)}, bf16[384,512]{1,0:T(8,128)(2,1)S(1)}, bf16[384,512]{1,0:T(8,128)(2,1)S(1)}, f32[4,8,128]{2,1,0:T(8,128)S(1)}) custom-call(f32[32]{0:T(128)S(1)} %broadcast_select_fusion.scale_ref, bf16[128,4096]{1,0:T(8,128)(2,1)S(1)} %bitcast.11, bf16[128,4096]{1,0:T(8,128)(2,1)S(1)} %bitcast.12, ...), custom_call_target="tpu_custom_call" | custom-call | flops 2415919104 | bytes 3145728 | tf_op jit(solution)/shard_map/attention/pallas_call | solution.py:64
  41.8 0.8 fusion
  42.6 1.3 collective-permute-start.2
  43.9 1.3 collective-permute-start.3
  45.5 9.3 %collective-permute-done.2 = bf16[128,1024]{1,0:T(8,128)(2,1)S(1)} collective-permute-done((bf16[128,1024]{1,0:T(8,128)(2,1)}, bf16[128,1024]{1,0:T(8,128)(2,1)S(1)}, u32[]{:S(2)}, u32[]{:S(2)}) %collective-permute-start.2) | collective-permute-done | bytes 262176 | tf_op jit(solution)/shard_map/ppermute | solution.py:349
  54.8 11.8 %collective-permute-done.3 = bf16[128,1024]{1,0:T(8,128)(2,1)} collective-permute-done((bf16[128,1024]{1,0:T(8,128)(2,1)}, bf16[128,1024]{1,0:T(8,128)(2,1)}, u32[]{:S(2)}, u32[]{:S(2)}) %collective-permute-start.3) | collective-permute-done | bytes 262176 | tf_op jit(solution)/shard_map/ppermute | solution.py:349
  66.6 1.1 add_convert_fusion
  67.9 104.2 %project.1 = (bf16[512,1024]{1,0:T(8,128)(2,1)S(1)}, f32[8,128]{1,0:T(8,128)S(1)}) custom-call(bf16[128,2560]{1,0:T(8,128)(2,1)S(1)} %pad_maximum_fusion.3.mine_ref, bf16[128,2560]{1,0:T(8,128)(2,1)S(1)} %pad_maximum_fusion.4.other_ref, f32[8,128]{1,0:T(8,128)S(1)} %scatter.4.term_ref, bf16[512,2560]{1,0:T(8,128)(2,1)} %pad_maximum_fusion.w0_ref, ...), custom_call_target="tpu_custom_call" | custom-call | flops 10737418240 | bytes 10485760 | tf_op jit(solution)/shard_map/project/pallas_call | solution.py:316
  172.1 0.5 multiply_bitcast_fusion
  172.6 1.0 copy.16
  (42 shorter events, 0.8 us)
Async XLA Ops:
  1.6 18.6 %collective-permute-start.1 = (bf16[128,1024]{1,0:T(8,128)(2,1)S(1)}, bf16[128,1024]{1,0:T(8,128)(2,1)S(1)}, u32[]{:S(2)}, u32[]{:S(2)}) collective-permute-start(bf16[128,1024]{1,0:T(8,128)(2,1)S(1)} %pad_maximum_fusion.5), channel_id=1, source_target_pairs={{0,8},{8,16},{16,24},{1,9},{9,17},{17,25},{2,10},{10,18},{18,26},{... | collective-permute-start | bytes 786440 | tf_op jit(solution)/shard_map/ppermute | solution.py:349
  6.6 13.6 %collective-permute-start = (bf16[128,1024]{1,0:T(8,128)(2,1)S(1)}, bf16[128,1024]{1,0:T(8,128)(2,1)S(1)}, u32[]{:S(2)}, u32[]{:S(2)}) collective-permute-start(bf16[128,1024]{1,0:T(8,128)(2,1)S(1)} %pad_maximum_fusion.5), channel_id=1, source_target_pairs={{0,16},{8,24},{1,17},{9,25},{2,18},{10,26},{3,19},{11,27},{4,20},{... | collective-permute-start | bytes 786440 | tf_op jit(solution)/shard_map/ppermute | solution.py:349
  11.1 2.6 %copy-start.6 = (bf16[512,512]{1,0:T(8,128)(2,1)S(1)}, bf16[512,512]{1,0:T(8,128)(2,1)}, u32[]{:S(2)}) copy-start(bf16[512,512]{1,0:T(8,128)(2,1)} %param.21) | copy-start | bytes 1572868
  11.1 2.6 %copy-start.7 = (bf16[512,512]{1,0:T(8,128)(2,1)S(1)}, bf16[512,512]{1,0:T(8,128)(2,1)}, u32[]{:S(2)}) copy-start(bf16[512,512]{1,0:T(8,128)(2,1)} %param.20) | copy-start | bytes 1572868
  13.8 1.3 copy-start.2
  16.6 51.3 %collective-permute-start.4 = (bf16[384,2560]{1,0:T(8,128)(2,1)}, bf16[384,2560]{1,0:T(8,128)(2,1)}, u32[]{:S(2)}, u32[]{:S(2)}) collective-permute-start(bf16[384,2560]{1,0:T(8,128)(2,1)} %slice.67), channel_id=1, source_target_pairs={{0,2},{1,3},{2,0},{3,1},{4,6},{5,7},{6,4},{7,5},{8,10},{9,11},{10,... | collective-permute-start | bytes 5898248 | tf_op jit(solution)/shard_map/ppermute | solution.py:353
  18.1 1.7 copy-start.8
  18.1 1.8 %copy-start.9 = (s32[8]{0:T(128)S(1)}, s32[8]{0:T(128)}, u32[]{:S(2)}) copy-start(s32[8]{0:T(128)} %param.18) | copy-start | bytes 100
  18.1 2.0 %copy-start.10 = (f32[32]{0:T(128)S(1)}, f32[32]{0:T(128)}, u32[]{:S(2)}) copy-start(f32[32]{0:T(128)} %param.17) | copy-start | bytes 388
  18.1 2.1 %copy-start.4 = (bf16[1,128,512]{2,1,0:T(8,128)(2,1)S(1)}, bf16[1,128,512]{2,1,0:T(8,128)(2,1)}, u32[]{:S(2)}) copy-start(bf16[1,128,512]{2,1,0:T(8,128)(2,1)} %param.14) | copy-start | bytes 393220
  18.1 2.1 %copy-start.5 = (bf16[1,128,512]{2,1,0:T(8,128)(2,1)S(1)}, bf16[1,128,512]{2,1,0:T(8,128)(2,1)}, u32[]{:S(2)}) copy-start(bf16[1,128,512]{2,1,0:T(8,128)(2,1)} %param.13) | copy-start | bytes 393220
  19.9 1.2 copy-start
  19.9 48.0 %collective-permute-start.5 = (bf16[512,2560]{1,0:T(8,128)(2,1)}, bf16[512,2560]{1,0:T(8,128)(2,1)}, u32[]{:S(2)}, u32[]{:S(2)}) collective-permute-start(bf16[512,2560]{1,0:T(8,128)(2,1)} %pad_maximum_fusion.w0_ref), channel_id=1, source_target_pairs={{0,1},{1,0},{2,3},{3,2},{4,5},{5,4},{6,7},{7,6},{8,9},{9,8},{10,11... | collective-permute-start | bytes 7864328 | tf_op jit(solution)/shard_map/ppermute | solution.py:353
  21.1 1.2 copy-start.1
  41.6 3.5 %copy-start.3 = (bf16[512,2048]{1,0:T(8,128)(2,1)S(1)}, bf16[512,2048]{1,0:T(8,128)(2,1)}, u32[]{:S(2)}) copy-start(bf16[512,2048]{1,0:T(8,128)(2,1)} %copy-done.2) | copy-start | bytes 6291460
  42.6 12.2 %collective-permute-start.2 = (bf16[128,1024]{1,0:T(8,128)(2,1)}, bf16[128,1024]{1,0:T(8,128)(2,1)S(1)}, u32[]{:S(2)}, u32[]{:S(2)}) collective-permute-start(bf16[128,1024]{1,0:T(8,128)(2,1)} %get-tuple-element.30), channel_id=1, source_target_pairs={{8,0},{16,8},{24,16},{9,1},{17,9},{25,17},{10,2},{18,10},{26,18},{... | collective-permute-start | bytes 786440 | tf_op jit(solution)/shard_map/ppermute | solution.py:349
  43.9 22.7 %collective-permute-start.3 = (bf16[128,1024]{1,0:T(8,128)(2,1)}, bf16[128,1024]{1,0:T(8,128)(2,1)}, u32[]{:S(2)}, u32[]{:S(2)}) collective-permute-start(bf16[128,1024]{1,0:T(8,128)(2,1)} %get-tuple-element.31), channel_id=1, source_target_pairs={{16,0},{24,8},{17,1},{25,9},{18,2},{26,10},{19,3},{27,11},{20,4},{... | collective-permute-start | bytes 786440 | tf_op jit(solution)/shard_map/ppermute | solution.py:349
